TPU v7x, 768 devices: a whole 4x8x12 slice. The times are simulated.
768 devices in a mesh: row: 8 (over y_lo, x), rep: 96 (over y_hi, z, core).
Axes of the slice: x: 4, y: 8 (y_hi: 4, y_lo: 2; y = y_hi * 2 + y_lo), z: 12, core: 2. Of those that a mesh axis runs over, the one named last changes fastest.
Arguments:
- features: bfloat16 [196608, 256], P(('row', 'rep')), may hold values from -6 to 6
- weight: bfloat16 [256, 256], replicated, may hold values from -0.375 to 0.375
- bias: float32 [256], replicated, may hold values from -3 to 3
- tile_vals: bfloat16 [8, 96, 32, 128, 128], P('row', 'rep'), may hold values from -0.25 to 0.25
- tile_rows: int32 [8, 96, 32], P('row', 'rep'), may hold values from 0 to 15, as said below
- tile_cols: int32 [8, 96, 32], P('row', 'rep'), may hold values from 0 to 15, as said below
- tile_counts: int32 [8, 96], P('row', 'rep'), may hold values from 1 to 32, as said below
- grad_out: bfloat16 [196608, 256], P(('row', 'rep')), may hold values from -6 to 6
Outputs:
- activations: bfloat16 [196608, 256], P(('row', 'rep'))
- grad_features: bfloat16 [196608, 256], P(('row', 'rep'))
- grad_weight: float32 [256, 256], replicated
- grad_bias: float32 [256], replicated
Inputs may be any that keep to these rules, and one draw needn't show every extreme that they name: `tile_rows`: destination tile indices; within one device the first tile_counts slots name distinct (tile_rows, tile_cols) pairs, and slots at or past tile_counts are unused. `tile_cols`: source tile indices. `tile_counts`: live slots per device; some device has all 32 slots live.
All inputs are finite; a program needn't handle non-finite values.
Results may differ from a plain program's by a relative error of at most 0.013.
Values may be sent and summed in bfloat16 or wider, within the bound.
No kernel may reach another device: no remote copies, remote signals or barrier semaphores. Data moves between devices by JAX's collectives and lax.ppermute only.
A program may use at most 32 MiB of HBM per device.

v0:
```python
import jax
import jax.numpy as jnp
from jax import lax
from jax.experimental import pallas as pl
from jax.experimental.pallas import tpu as pltpu
from jax.sharding import PartitionSpec as P

K = 8
Z = 12
ORDER = (0, 2, 1, 3)
BF = jnp.bfloat16
F32 = jnp.float32


def forward_tiles(rows, cols, count, vals, source, even, odd, acc):
    acc[...] = jnp.zeros_like(acc)
    live = count[0]
    for t in range(vals.shape[0]):
        product = jnp.dot(vals[t], source[cols[t]], preferred_element_type=F32)
        acc[rows[t]] += jnp.where(t < live, product, 0.0)
    tile = vals.shape[1]
    for o in range(K):
        for h in range(2):
            part = acc[2 * o + h].astype(BF)
            target = odd if o % 2 else even
            target[o // 2, h * tile : (h + 1) * tile, :] = part


def backward_tiles(rows, cols, count, core, vals, own, other, far, out, acc, reach):
    slots, tile = vals.shape[:2]
    step = 2 * core[0]
    for k in range(4):
        for h in range(2):
            span = slice(h * tile, (h + 1) * tile)
            reach[2 * k + h] = own[ORDER[k], span, :]
            reach[8 + 2 * k + h] = other[ORDER[k], span, :]
    for h in range(2):
        reach[16 + h] = far[h * tile : (h + 1) * tile, :]
    acc[...] = jnp.zeros_like(acc)
    live = count[0]
    for t in range(slots):
        row = rows[t]
        place = (row // 4) * 2 + row % 2
        place = jnp.where(row % 4 >= 2, place + 8 + step, place)
        product = lax.dot_general(
            vals[t], reach[place], (((0,), (0,)), ((), ())), preferred_element_type=F32
        )
        acc[cols[t]] += jnp.where(t < live, product, 0.0)
    for j in range(out.shape[0]):
        for h in range(2):
            out[j, h * tile : (h + 1) * tile, :] = acc[2 * j + h].astype(BF)


def tiles_call(kernel, scalars, vals, arrays, outs, extra=()):
    slots, tile = vals.shape[0], vals.shape[1]
    width = arrays[0].shape[-1]
    smem = pl.BlockSpec(memory_space=pltpu.SMEM)
    vmem = pl.BlockSpec(memory_space=pltpu.VMEM)
    return pl.pallas_call(
        kernel,
        out_shape=outs,
        in_specs=[smem] * len(scalars) + [vmem] * (1 + len(arrays)),
        out_specs=jax.tree.map(lambda _: vmem, outs),
        scratch_shapes=[pltpu.VMEM((2 * K, tile, width), F32), *extra],
        compiler_params=pltpu.CompilerParams(vmem_limit_bytes=24 * 1024 * 1024),
        cost_estimate=pl.CostEstimate(
            flops=2 * slots * tile * tile * width, bytes_accessed=3 << 20, transcendentals=0
        ),
    )(*scalars, vals, *arrays)


def passed(shard, axis, to):
    size = lax.axis_size(axis)
    pairs = [(i, to(i)) for i in range(size)]
    return lax.ppermute(shard, axis, [(i, j % size) for i, j in pairs if j is not None])


def gathered(shard, axis, groups=None):
    size = lax.axis_size(axis) if groups is None else len(groups[0])
    copies = jnp.broadcast_to(shard[None], (size,) + shard.shape)
    return lax.all_to_all(copies, axis, 0, 0, axis_index_groups=groups)


def summed(shard, axis, groups=None):
    return jnp.sum(gathered(shard, axis, groups).astype(F32), axis=0)


def depth(i, by):
    return i // (2 * Z) * (2 * Z) + (i + 2 * by) % (2 * Z)


def plane_groups(z_chips):
    rows, reps = lax.axis_size("row"), lax.axis_size("rep")
    return [
        [r * reps + y + i for r in range(rows) for y in range(0, reps, 2 * z_chips)]
        for i in range(2 * z_chips)
    ]


def shards(features, weight, bias, tile_vals, tile_rows, tile_cols, tile_counts, grad_out):
    block, width = features.shape
    vals = tile_vals[0, 0]
    rows = tile_rows[0, 0]
    cols = tile_cols[0, 0]
    count = tile_counts[0]
    tile = vals.shape[1]
    group_rows = lax.axis_size("row")
    core = (lax.axis_index("rep") % 2).astype(jnp.int32)
    wide = jax.ShapeDtypeStruct((K // 2, block, width), BF)

    with jax.named_scope("gather_features"):
        source = gathered(features, "row").reshape(group_rows * block // tile, tile, width)
    with jax.named_scope("forward_tiles"):
        even, odd = tiles_call(
            forward_tiles, [rows, cols, count], vals, [source], (wide, wide)
        )
    with jax.named_scope("window_sum"):
        far = passed(odd[3], "rep", lambda i: i + 3 if i % 2 else None)
        other = passed(odd, "rep", lambda i: i ^ 1)
        shifted = jnp.concatenate([jnp.zeros_like(other[:1]), other[:3]])
        sums = even.astype(F32) + jnp.where(core == 0, shifted, other).astype(F32)
        ahead = passed(sums[3].astype(BF), "rep", lambda i: i + 2)
        behind = passed(sums[1].astype(BF), "rep", lambda i: i - 2)
        middle = sums[2] + far.astype(F32) + ahead.astype(F32) + behind.astype(F32)
        aggregate = sums[0] + passed(middle.astype(BF), "rep", lambda i: i + 4).astype(F32)
    with jax.named_scope("pointwise"):
        top = aggregate.astype(BF)
        rest = (aggregate - top.astype(F32)).astype(BF)
        pre = (
            jnp.dot(top, weight, preferred_element_type=F32)
            + jnp.dot(rest, weight, preferred_element_type=F32)
            + bias[None, :]
        )
        activations = jax.nn.silu(pre).astype(BF)
        sig = jax.nn.sigmoid(pre)
        grad_pre = (grad_out.astype(F32) * sig * (1.0 + pre * (1.0 - sig))).astype(BF)
        local_weight = lax.dot_general(
            top, grad_pre, (((0,), (0,)), ((), ())), preferred_element_type=F32
        )
        local_bias = jnp.sum(grad_pre.astype(F32), axis=0)
    with jax.named_scope("weight_sum_plane"):
        plane = plane_groups(Z)
        members = len(plane[0])
        piece = width // members
        parts = local_weight.reshape(members, piece, width).astype(BF)
        parts = lax.all_to_all(parts, ("row", "rep"), 0, 0, axis_index_groups=plane)
        part = jnp.sum(parts.astype(F32), axis=0)
        part = jnp.concatenate([part, local_bias[None], jnp.zeros((15 - piece, width), F32)])
    with jax.named_scope("window_gather"):
        second = passed(grad_pre, "rep", lambda i: i - 4)
        far = passed(grad_pre, "rep", lambda i: i - 7 if i % 2 == 0 else None)
        second, far, part = lax.optimization_barrier((second, far, part))
        near = passed(jnp.concatenate([grad_pre, second]), "rep", lambda i: i - 2)
        sent = part.astype(BF)
        for by in (1, -1, 2):
            part = part + passed(sent, "rep", lambda i: depth(i, by)).astype(F32)
        near, part = lax.optimization_barrier((near, part))
        own = jnp.concatenate([grad_pre, second, near]).reshape(4, block, width)
        given = jnp.concatenate([own.reshape(4 * block, width), part.astype(BF)])
        other = passed(given, "rep", lambda i: i ^ 1)
        part = part + other[4 * block :].astype(F32)
        other = other[: 4 * block].reshape(4, block, width)
    with jax.named_scope("backward_tiles"):
        terms = tiles_call(
            backward_tiles,
            [rows, cols, count, core[None]],
            vals,
            [own, other, far],
            jax.ShapeDtypeStruct((group_rows, block, width), BF),
            [pltpu.VMEM((2 * K + 2, tile, width), BF)],
        )
        _, part = lax.optimization_barrier((terms, part))
    with jax.named_scope("weight_sum_depth"):
        sent = part.astype(BF)
        for by in (4, -4):
            part = part + passed(sent, "rep", lambda i: depth(i, by)).astype(F32)
    with jax.named_scope("source_sum"):
        arrived = lax.all_to_all(terms, "row", 0, 0)
        source_grad = jnp.sum(arrived.astype(F32), axis=0).astype(BF)
        grad_features = lax.dot_general(
            source_grad, weight, (((1,), (1,)), ((), ())), preferred_element_type=F32
        ).astype(BF)
    with jax.named_scope("weight_gather"):
        part, _ = lax.optimization_barrier((part.astype(BF), arrived))
        pieces = gathered(part, ("row", "rep"), plane)
        grad_weight = pieces[:, :piece].reshape(width, width).astype(F32)
        grad_bias = jnp.sum(pieces[:, piece].astype(F32), axis=0)
    return (activations, grad_features, grad_weight, grad_bias)


def solution(mesh):
    placed = (
        P(("row", "rep"), None),
        P(),
        P(),
        P("row", "rep", None, None, None),
        P("row", "rep", None),
        P("row", "rep", None),
        P("row", "rep"),
        P(("row", "rep"), None),
    )
    return jax.shard_map(
        shards,
        mesh=mesh,
        in_specs=placed,
        out_specs=(P(("row", "rep"), None), P(("row", "rep"), None), P(), P()),
        check_vma=False,
    )
```

profile of v0, /device:TPU:1, one launch (start us, length us, event | category | flops | bytes accessed | tf_op | source)
XLA Modules:
  0.0 154.6 jit_solution(3069900978886011262)
XLA Ops:
  0.6 2.0 %broadcast_in_dim.10 = bf16[8,256,256]{2,1,0:T(8,128)(2,1)} broadcast(bf16[256,256]{1,0:T(8,128)(2,1)} %param.8), dimensions={1,2} | broadcast | bytes 1179648 | tf_op jit(solution)/shard_map/gather_features/broadcast_in_dim | solution.py:80
  2.7 6.0 %all-to-all-start = ((bf16[8,256,256]{2,1,0:T(8,128)(2,1)}), bf16[8,256,256]{2,1,0:T(8,128)(2,1)S(1)}, u32[]{:S(2)}, u32[]{:S(2)}) async-start(bf16[8,256,256]{2,1,0:T(8,128)(2,1)} %broadcast_in_dim.10), calls=%async_computation | async-start | bytes 2097152 | tf_op jit(solution)/shard_map/gather_features/all_to_all | solution.py:81
  9.3 8.8 %all-to-all-done = bf16[8,256,256]{2,1,0:T(8,128)(2,1)S(1)} async-done(((bf16[8,256,256]{2,1,0:T(8,128)(2,1)}), bf16[8,256,256]{2,1,0:T(8,128)(2,1)S(1)}, u32[]{:S(2)}, u32[]{:S(2)}) %all-to-all-start) | async-done | bytes 1048608 | tf_op jit(solution)/shard_map/gather_features/all_to_all | solution.py:81
  18.1 1.5 forward_tiles.1
  19.6 11.2 %collective-permute-start = (bf16[4,256,256]{2,1,0:T(8,128)(2,1)S(1)}, bf16[4,256,256]{2,1,0:T(8,128)(2,1)S(1)}, u32[]{:S(2)}, u32[]{:S(2)}) collective-permute-start(bf16[4,256,256]{2,1,0:T(8,128)(2,1)S(1)} %get-tuple-element.14), channel_id=1, source_target_pairs={{0,1},{1,0},{2,3},{3,2},{4,5},{5,4},{6,7},{7,6},{8,9},{9,8},{10,11... | collective-permute-start | bytes 1572872 | tf_op jit(solution)/shard_map/window_sum/ppermute | solution.py:75
  30.8 2.7 %collective-permute-start.1 = (bf16[256,256]{1,0:T(8,128)(2,1)S(1)}, bf16[256,256]{1,0:T(8,128)(2,1)S(1)}, u32[]{:S(2)}, u32[]{:S(2)}) collective-permute-start(bf16[256,256]{1,0:T(8,128)(2,1)S(1)} %slice_bitcast_fusion.5), channel_id=1, source_target_pairs={{1,4},{3,6},{5,8},{7,10},{9,12},{11,14},{13,16},{15,18},{17,20},{1... | collective-permute-start | bytes 393224 | tf_op jit(solution)/shard_map/window_sum/ppermute | solution.py:75
  33.8 4.0 %collective-permute-start.2 = (bf16[256,256]{1,0:T(8,128)(2,1)S(1)}, bf16[256,256]{1,0:T(8,128)(2,1)S(1)}, u32[]{:S(2)}, u32[]{:S(2)}) collective-permute-start(bf16[256,256]{1,0:T(8,128)(2,1)S(1)} %get-tuple-element.26), channel_id=1, source_target_pairs={{0,2},{1,3},{2,4},{3,5},{4,6},{5,7},{6,8},{7,9},{8,10},{9,11},{10,... | collective-permute-start | bytes 393224 | tf_op jit(solution)/shard_map/window_sum/ppermute | solution.py:75
  37.8 10.8 %collective-permute-start.3 = (bf16[256,256]{1,0:T(8,128)(2,1)S(1)}, bf16[256,256]{1,0:T(8,128)(2,1)S(1)}, u32[]{:S(2)}, u32[]{:S(2)}) collective-permute-start(bf16[256,256]{1,0:T(8,128)(2,1)S(1)} %get-tuple-element.27), channel_id=1, source_target_pairs={{0,94},{1,95},{2,0},{3,1},{4,2},{5,3},{6,4},{7,5},{8,6},{9,7},{10,... | collective-permute-start | bytes 393224 | tf_op jit(solution)/shard_map/window_sum/ppermute | solution.py:75
  48.6 4.9 %collective-permute-done.2 = bf16[256,256]{1,0:T(8,128)(2,1)S(1)} collective-permute-done((bf16[256,256]{1,0:T(8,128)(2,1)S(1)}, bf16[256,256]{1,0:T(8,128)(2,1)S(1)}, u32[]{:S(2)}, u32[]{:S(2)}) %collective-permute-start.2) | collective-permute-done | bytes 131104 | tf_op jit(solution)/shard_map/window_sum/ppermute | solution.py:75
  53.6 1.9 %collective-permute-start.4 = (bf16[256,256]{1,0:T(8,128)(2,1)S(1)}, bf16[256,256]{1,0:T(8,128)(2,1)S(1)}, u32[]{:S(2)}, u32[]{:S(2)}) collective-permute-start(bf16[256,256]{1,0:T(8,128)(2,1)S(1)} %fusion.5), channel_id=1, source_target_pairs={{0,4},{1,5},{2,6},{3,7},{4,8},{5,9},{6,10},{7,11},{8,12},{9,13},{1... | collective-permute-start | bytes 393224 | tf_op jit(solution)/shard_map/window_sum/ppermute | solution.py:75
  55.5 10.2 %collective-permute-done.4 = bf16[256,256]{1,0:T(8,128)(2,1)S(1)} collective-permute-done((bf16[256,256]{1,0:T(8,128)(2,1)S(1)}, bf16[256,256]{1,0:T(8,128)(2,1)S(1)}, u32[]{:S(2)}, u32[]{:S(2)}) %collective-permute-start.4) | collective-permute-done | bytes 131104 | tf_op jit(solution)/shard_map/window_sum/ppermute | solution.py:75
  67.8 8.2 %all-to-all-start.1 = ((bf16[32,8,256]{2,1,0:T(8,128)(2,1)}), bf16[32,8,256]{2,1,0:T(8,128)(2,1)S(1)}, u32[]{:S(2)}, u32[]{:S(2)}) async-start(bf16[32,8,256]{2,1,0:T(8,128)(2,1)} %fusion.1), calls=%async_computation.1 | async-start | bytes 262144 | tf_op jit(solution)/shard_map/weight_sum_plane/all_to_all | solution.py:146
  76.1 1.3 collective-permute-start.6
  77.4 1.9 %collective-permute-start.5 = (bf16[256,256]{1,0:T(8,128)(2,1)S(1)}, bf16[256,256]{1,0:T(8,128)(2,1)S(1)}, u32[]{:S(2)}, u32[]{:S(2)}) collective-permute-start(bf16[256,256]{1,0:T(8,128)(2,1)S(1)} %get-tuple-element.23), channel_id=1, source_target_pairs={{0,92},{1,93},{2,94},{3,95},{4,0},{5,1},{6,2},{7,3},{8,4},{9,5},{1... | collective-permute-start | bytes 393224 | tf_op jit(solution)/shard_map/window_gather/ppermute | solution.py:75
  79.3 5.9 %all-to-all-done.1 = bf16[32,8,256]{2,1,0:T(8,128)(2,1)S(1)} async-done(((bf16[32,8,256]{2,1,0:T(8,128)(2,1)}), bf16[32,8,256]{2,1,0:T(8,128)(2,1)S(1)}, u32[]{:S(2)}, u32[]{:S(2)}) %all-to-all-start.1) | async-done | bytes 131104 | tf_op jit(solution)/shard_map/weight_sum_plane/all_to_all | solution.py:146
  85.3 3.8 %collective-permute-done.6.far = bf16[256,256]{1,0:T(8,128)(2,1)S(1)} collective-permute-done((bf16[256,256]{1,0:T(8,128)(2,1)S(1)}, bf16[256,256]{1,0:T(8,128)(2,1)S(1)}, u32[]{:S(2)}, u32[]{:S(2)}) %collective-permute-start.6) | collective-permute-done | bytes 131104 | tf_op jit(solution)/shard_map/window_gather/ppermute | solution.py:75
  89.1 3.4 %collective-permute-done.5 = bf16[256,256]{1,0:T(8,128)(2,1)S(1)} collective-permute-done((bf16[256,256]{1,0:T(8,128)(2,1)S(1)}, bf16[256,256]{1,0:T(8,128)(2,1)S(1)}, u32[]{:S(2)}, u32[]{:S(2)}) %collective-permute-start.5) | collective-permute-done | bytes 131104 | tf_op jit(solution)/shard_map/window_gather/ppermute | solution.py:75
  92.5 2.9 %collective-permute-start.7 = (bf16[512,256]{1,0:T(8,128)(2,1)S(1)}, bf16[512,256]{1,0:T(8,128)(2,1)S(1)}, u32[]{:S(2)}, u32[]{:S(2)}) collective-permute-start(bf16[512,256]{1,0:T(8,128)(2,1)S(1)} %pad_maximum_fusion.2), channel_id=1, source_target_pairs={{0,94},{1,95},{2,0},{3,1},{4,2},{5,3},{6,4},{7,5},{8,6},{9,7},{10,... | collective-permute-start | bytes 786440 | tf_op jit(solution)/shard_map/window_gather/ppermute | solution.py:75
  95.4 1.9 %collective-permute-start.10 = (bf16[16,256]{1,0:T(8,128)(2,1)S(1)}, bf16[16,256]{1,0:T(8,128)(2,1)S(1)}, u32[]{:S(2)}, u32[]{:S(2)}) collective-permute-start(bf16[16,256]{1,0:T(8,128)(2,1)S(1)} %convert_element_type.123), channel_id=1, source_target_pairs={{0,4},{1,5},{2,6},{3,7},{4,8},{5,9},{6,10},{7,11},{8,12},{9,13},{1... | collective-permute-start | bytes 24584 | tf_op jit(solution)/shard_map/window_gather/ppermute | solution.py:75
  97.3 4.8 %collective-permute-start.9 = (bf16[16,256]{1,0:T(8,128)(2,1)S(1)}, bf16[16,256]{1,0:T(8,128)(2,1)S(1)}, u32[]{:S(2)}, u32[]{:S(2)}) collective-permute-start(bf16[16,256]{1,0:T(8,128)(2,1)S(1)} %convert_element_type.123), channel_id=1, source_target_pairs={{0,22},{1,23},{2,0},{3,1},{4,2},{5,3},{6,4},{7,5},{8,6},{9,7},{10,... | collective-permute-start | bytes 24584 | tf_op jit(solution)/shard_map/window_gather/ppermute | solution.py:75
  102.1 1.9 %collective-permute-start.8 = (bf16[16,256]{1,0:T(8,128)(2,1)S(1)}, bf16[16,256]{1,0:T(8,128)(2,1)S(1)}, u32[]{:S(2)}, u32[]{:S(2)}) collective-permute-start(bf16[16,256]{1,0:T(8,128)(2,1)S(1)} %convert_element_type.123), channel_id=1, source_target_pairs={{0,2},{1,3},{2,4},{3,5},{4,6},{5,7},{6,8},{7,9},{8,10},{9,11},{10,... | collective-permute-start | bytes 24584 | tf_op jit(solution)/shard_map/window_gather/ppermute | solution.py:75
  104.0 3.7 %collective-permute-done.8 = bf16[16,256]{1,0:T(8,128)(2,1)S(1)} collective-permute-done((bf16[16,256]{1,0:T(8,128)(2,1)S(1)}, bf16[16,256]{1,0:T(8,128)(2,1)S(1)}, u32[]{:S(2)}, u32[]{:S(2)}) %collective-permute-start.8) | collective-permute-done | bytes 8224 | tf_op jit(solution)/shard_map/window_gather/ppermute | solution.py:75
  107.8 4.6 %collective-permute-start.11 = (bf16[1040,256]{1,0:T(8,128)(2,1)S(1)}, bf16[1040,256]{1,0:T(8,128)(2,1)S(1)}, u32[]{:S(2)}, u32[]{:S(2)}) collective-permute-start(bf16[1040,256]{1,0:T(8,128)(2,1)S(1)} %pad_maximum_fusion), channel_id=1, source_target_pairs={{0,1},{1,0},{2,3},{3,2},{4,5},{5,4},{6,7},{7,6},{8,9},{9,8},{10,11... | collective-permute-start | bytes 1597448 | tf_op jit(solution)/shard_map/window_gather/ppermute | solution.py:75
  112.4 1.5 collective-permute-done.11
  113.9 2.6 %backward_tiles.1 = bf16[8,256,256]{2,1,0:T(8,128)(2,1)} custom-call(s32[32]{0:T(128)S(1)} %bitcast.56, s32[32]{0:T(128)S(1)} %bitcast.58, s32[1]{0:T(128)} %bitcast.49.count, s32[1]{0:T(128)} %bitcast.10.core, bf16[32,128,128]{2,1,0:T(8,128)(2,1)S(1)} %bitcast.52, bf16[4,256,256]{2,1,0:T(8,128)(2,1)S(1)} %bitcast.53, bf16[4,256,256]{2,1,0:T(8,128)(2,1)S(1)} %bitcast.54, ...), custom_call_target="tpu_custom_call" | custom-call | flops 268435456 | bytes 3145728 | tf_op jit(solution)/shard_map/backward_tiles/pallas_call | solution.py:59
  116.5 4.2 %all-to-all-start.2 = ((bf16[8,256,256]{2,1,0:T(8,128)(2,1)}), bf16[8,256,256]{2,1,0:T(8,128)(2,1)S(1)}, u32[]{:S(2)}, u32[]{:S(2)}) async-start(bf16[8,256,256]{2,1,0:T(8,128)(2,1)} %backward_tiles.1), calls=%async_computation.2 | async-start | bytes 2097152 | tf_op jit(solution)/shard_map/source_sum/all_to_all | solution.py:178
  120.7 3.1 %collective-permute-start.13 = (bf16[16,256]{1,0:T(8,128)(2,1)S(1)}, bf16[16,256]{1,0:T(8,128)(2,1)S(1)}, u32[]{:S(2)}, u32[]{:S(2)}) collective-permute-start(bf16[16,256]{1,0:T(8,128)(2,1)S(1)} %convert_element_type.130), channel_id=1, source_target_pairs={{0,16},{1,17},{2,18},{3,19},{4,20},{5,21},{6,22},{7,23},{8,0},{9,1... | collective-permute-start | bytes 24584 | tf_op jit(solution)/shard_map/weight_sum_depth/ppermute | solution.py:75
  123.8 6.1 %collective-permute-start.12 = (bf16[16,256]{1,0:T(8,128)(2,1)S(1)}, bf16[16,256]{1,0:T(8,128)(2,1)S(1)}, u32[]{:S(2)}, u32[]{:S(2)}) collective-permute-start(bf16[16,256]{1,0:T(8,128)(2,1)S(1)} %convert_element_type.130), channel_id=1, source_target_pairs={{0,8},{1,9},{2,10},{3,11},{4,12},{5,13},{6,14},{7,15},{8,16},{9,17... | collective-permute-start | bytes 24584 | tf_op jit(solution)/shard_map/weight_sum_depth/ppermute | solution.py:75
  129.9 2.2 %collective-permute-done.12 = bf16[16,256]{1,0:T(8,128)(2,1)S(1)} collective-permute-done((bf16[16,256]{1,0:T(8,128)(2,1)S(1)}, bf16[16,256]{1,0:T(8,128)(2,1)S(1)}, u32[]{:S(2)}, u32[]{:S(2)}) %collective-permute-start.12) | collective-permute-done | bytes 8224 | tf_op jit(solution)/shard_map/weight_sum_depth/ppermute | solution.py:75
  132.1 3.5 %all-to-all-done.2 = bf16[8,256,256]{2,1,0:T(8,128)(2,1)S(1)} async-done(((bf16[8,256,256]{2,1,0:T(8,128)(2,1)}), bf16[8,256,256]{2,1,0:T(8,128)(2,1)S(1)}, u32[]{:S(2)}, u32[]{:S(2)}) %all-to-all-start.2) | async-done | bytes 1048608 | tf_op jit(solution)/shard_map/source_sum/all_to_all | solution.py:178
  136.3 6.7 %all-to-all-start.3 = ((bf16[32,16,256]{2,1,0:T(8,128)(2,1)}), bf16[32,16,256]{2,1,0:T(8,128)(2,1)S(1)}, u32[]{:S(2)}, u32[]{:S(2)}) async-start(bf16[32,16,256]{2,1,0:T(8,128)(2,1)} %broadcast_in_dim.27), calls=%async_computation.3 | async-start | bytes 524288 | tf_op jit(solution)/shard_map/weight_gather/all_to_all | solution.py:81
  144.1 9.2 %all-to-all-done.3 = bf16[32,16,256]{2,1,0:T(8,128)(2,1)S(1)} async-done(((bf16[32,16,256]{2,1,0:T(8,128)(2,1)}), bf16[32,16,256]{2,1,0:T(8,128)(2,1)S(1)}, u32[]{:S(2)}, u32[]{:S(2)}) %all-to-all-start.3) | async-done | bytes 262176 | tf_op jit(solution)/shard_map/weight_gather/all_to_all | solution.py:81
  (47 shorter events, 5.8 us)
Async XLA Ops:
  0.6 65.1 %copy-start = (bf16[256,256]{1,0:T(8,128)(2,1)S(1)}, bf16[256,256]{1,0:T(8,128)(2,1)}, u32[]{:S(2)}) copy-start(bf16[256,256]{1,0:T(8,128)(2,1)} %param.9) | copy-start | bytes 393220
  2.6 15.5 %copy-start.1 = (bf16[1,1,32,128,128]{4,3,2,1,0:T(8,128)(2,1)S(1)}, bf16[1,1,32,128,128]{4,3,2,1,0:T(8,128)(2,1)}, u32[]{:S(2)}) copy-start(bf16[1,1,32,128,128]{4,3,2,1,0:T(8,128)(2,1)} %param.11) | copy-start | bytes 3145732
  2.6 15.5 %copy-start.2 = (s32[1,1,32]{2,1,0:T(1,128)S(1)}, s32[1,1,32]{2,1,0:T(1,128)}, u32[]{:S(2)}) copy-start(s32[1,1,32]{2,1,0:T(1,128)} %param.12) | copy-start | bytes 388
  2.6 15.5 %copy-start.3 = (s32[1,1,32]{2,1,0:T(1,128)S(1)}, s32[1,1,32]{2,1,0:T(1,128)}, u32[]{:S(2)}) copy-start(s32[1,1,32]{2,1,0:T(1,128)} %param.13) | copy-start | bytes 388
  2.7 15.4 %all-to-all-start = ((bf16[8,256,256]{2,1,0:T(8,128)(2,1)}), bf16[8,256,256]{2,1,0:T(8,128)(2,1)S(1)}, u32[]{:S(2)}, u32[]{:S(2)}) async-start(bf16[8,256,256]{2,1,0:T(8,128)(2,1)} %broadcast_in_dim.10), calls=%async_computation | async-start | bytes 2097152 | tf_op jit(solution)/shard_map/gather_features/all_to_all | solution.py:81
  19.6 14.0 %collective-permute-start = (bf16[4,256,256]{2,1,0:T(8,128)(2,1)S(1)}, bf16[4,256,256]{2,1,0:T(8,128)(2,1)S(1)}, u32[]{:S(2)}, u32[]{:S(2)}) collective-permute-start(bf16[4,256,256]{2,1,0:T(8,128)(2,1)S(1)} %get-tuple-element.14), channel_id=1, source_target_pairs={{0,1},{1,0},{2,3},{3,2},{4,5},{5,4},{6,7},{7,6},{8,9},{9,8},{10,11... | collective-permute-start | bytes 1572872 | tf_op jit(solution)/shard_map/window_sum/ppermute | solution.py:75
  30.8 17.8 %collective-permute-start.1 = (bf16[256,256]{1,0:T(8,128)(2,1)S(1)}, bf16[256,256]{1,0:T(8,128)(2,1)S(1)}, u32[]{:S(2)}, u32[]{:S(2)}) collective-permute-start(bf16[256,256]{1,0:T(8,128)(2,1)S(1)} %slice_bitcast_fusion.5), channel_id=1, source_target_pairs={{1,4},{3,6},{5,8},{7,10},{9,12},{11,14},{13,16},{15,18},{17,20},{1... | collective-permute-start | bytes 393224 | tf_op jit(solution)/shard_map/window_sum/ppermute | solution.py:75
  33.8 19.7 %collective-permute-start.2 = (bf16[256,256]{1,0:T(8,128)(2,1)S(1)}, bf16[256,256]{1,0:T(8,128)(2,1)S(1)}, u32[]{:S(2)}, u32[]{:S(2)}) collective-permute-start(bf16[256,256]{1,0:T(8,128)(2,1)S(1)} %get-tuple-element.26), channel_id=1, source_target_pairs={{0,2},{1,3},{2,4},{3,5},{4,6},{5,7},{6,8},{7,9},{8,10},{9,11},{10,... | collective-permute-start | bytes 393224 | tf_op jit(solution)/shard_map/window_sum/ppermute | solution.py:75
  37.8 15.7 %collective-permute-start.3 = (bf16[256,256]{1,0:T(8,128)(2,1)S(1)}, bf16[256,256]{1,0:T(8,128)(2,1)S(1)}, u32[]{:S(2)}, u32[]{:S(2)}) collective-permute-start(bf16[256,256]{1,0:T(8,128)(2,1)S(1)} %get-tuple-element.27), channel_id=1, source_target_pairs={{0,94},{1,95},{2,0},{3,1},{4,2},{5,3},{6,4},{7,5},{8,6},{9,7},{10,... | collective-permute-start | bytes 393224 | tf_op jit(solution)/shard_map/window_sum/ppermute | solution.py:75
  53.5 12.5 %copy-start.4 = (bf16[256,256]{1,0:T(8,128)(2,1)S(1)}, bf16[256,256]{1,0:T(8,128)(2,1)}, u32[]{:S(2)}) copy-start(bf16[256,256]{1,0:T(8,128)(2,1)} %param.15) | copy-start | bytes 393220
  53.5 12.5 %copy-start.5 = (f32[256]{0:T(256)S(1)}, f32[256]{0:T(256)}, u32[]{:S(2)}) copy-start(f32[256]{0:T(256)} %param.10) | copy-start | bytes 3076
  53.6 12.2 %collective-permute-start.4 = (bf16[256,256]{1,0:T(8,128)(2,1)S(1)}, bf16[256,256]{1,0:T(8,128)(2,1)S(1)}, u32[]{:S(2)}, u32[]{:S(2)}) collective-permute-start(bf16[256,256]{1,0:T(8,128)(2,1)S(1)} %fusion.5), channel_id=1, source_target_pairs={{0,4},{1,5},{2,6},{3,7},{4,8},{5,9},{6,10},{7,11},{8,12},{9,13},{1... | collective-permute-start | bytes 393224 | tf_op jit(solution)/shard_map/window_sum/ppermute | solution.py:75
  67.8 17.3 %all-to-all-start.1 = ((bf16[32,8,256]{2,1,0:T(8,128)(2,1)}), bf16[32,8,256]{2,1,0:T(8,128)(2,1)S(1)}, u32[]{:S(2)}, u32[]{:S(2)}) async-start(bf16[32,8,256]{2,1,0:T(8,128)(2,1)} %fusion.1), calls=%async_computation.1 | async-start | bytes 262144 | tf_op jit(solution)/shard_map/weight_sum_plane/all_to_all | solution.py:146
  76.1 13.0 %collective-permute-start.6 = (bf16[256,256]{1,0:T(8,128)(2,1)S(1)}, bf16[256,256]{1,0:T(8,128)(2,1)S(1)}, u32[]{:S(2)}, u32[]{:S(2)}) collective-permute-start(bf16[256,256]{1,0:T(8,128)(2,1)S(1)} %get-tuple-element.23), channel_id=1, source_target_pairs={{0,89},{2,91},{4,93},{6,95},{8,1},{10,3},{12,5},{14,7},{16,9},{18,... | collective-permute-start | bytes 393224 | tf_op jit(solution)/shard_map/window_gather/ppermute | solution.py:75
  77.4 15.0 %collective-permute-start.5 = (bf16[256,256]{1,0:T(8,128)(2,1)S(1)}, bf16[256,256]{1,0:T(8,128)(2,1)S(1)}, u32[]{:S(2)}, u32[]{:S(2)}) collective-permute-start(bf16[256,256]{1,0:T(8,128)(2,1)S(1)} %get-tuple-element.23), channel_id=1, source_target_pairs={{0,92},{1,93},{2,94},{3,95},{4,0},{5,1},{6,2},{7,3},{8,4},{9,5},{1... | collective-permute-start | bytes 393224 | tf_op jit(solution)/shard_map/window_gather/ppermute | solution.py:75
  92.5 15.2 %collective-permute-start.7 = (bf16[512,256]{1,0:T(8,128)(2,1)S(1)}, bf16[512,256]{1,0:T(8,128)(2,1)S(1)}, u32[]{:S(2)}, u32[]{:S(2)}) collective-permute-start(bf16[512,256]{1,0:T(8,128)(2,1)S(1)} %pad_maximum_fusion.2), channel_id=1, source_target_pairs={{0,94},{1,95},{2,0},{3,1},{4,2},{5,3},{6,4},{7,5},{8,6},{9,7},{10,... | collective-permute-start | bytes 786440 | tf_op jit(solution)/shard_map/window_gather/ppermute | solution.py:75
  95.4 8.7 %collective-permute-start.10 = (bf16[16,256]{1,0:T(8,128)(2,1)S(1)}, bf16[16,256]{1,0:T(8,128)(2,1)S(1)}, u32[]{:S(2)}, u32[]{:S(2)}) collective-permute-start(bf16[16,256]{1,0:T(8,128)(2,1)S(1)} %convert_element_type.123), channel_id=1, source_target_pairs={{0,4},{1,5},{2,6},{3,7},{4,8},{5,9},{6,10},{7,11},{8,12},{9,13},{1... | collective-permute-start | bytes 24584 | tf_op jit(solution)/shard_map/window_gather/ppermute | solution.py:75
  97.3 6.7 %collective-permute-start.9 = (bf16[16,256]{1,0:T(8,128)(2,1)S(1)}, bf16[16,256]{1,0:T(8,128)(2,1)S(1)}, u32[]{:S(2)}, u32[]{:S(2)}) collective-permute-start(bf16[16,256]{1,0:T(8,128)(2,1)S(1)} %convert_element_type.123), channel_id=1, source_target_pairs={{0,22},{1,23},{2,0},{3,1},{4,2},{5,3},{6,4},{7,5},{8,6},{9,7},{10,... | collective-permute-start | bytes 24584 | tf_op jit(solution)/shard_map/window_gather/ppermute | solution.py:75
  102.1 5.6 %collective-permute-start.8 = (bf16[16,256]{1,0:T(8,128)(2,1)S(1)}, bf16[16,256]{1,0:T(8,128)(2,1)S(1)}, u32[]{:S(2)}, u32[]{:S(2)}) collective-permute-start(bf16[16,256]{1,0:T(8,128)(2,1)S(1)} %convert_element_type.123), channel_id=1, source_target_pairs={{0,2},{1,3},{2,4},{3,5},{4,6},{5,7},{6,8},{7,9},{8,10},{9,11},{10,... | collective-permute-start | bytes 24584 | tf_op jit(solution)/shard_map/window_gather/ppermute | solution.py:75
  107.8 6.1 %collective-permute-start.11 = (bf16[1040,256]{1,0:T(8,128)(2,1)S(1)}, bf16[1040,256]{1,0:T(8,128)(2,1)S(1)}, u32[]{:S(2)}, u32[]{:S(2)}) collective-permute-start(bf16[1040,256]{1,0:T(8,128)(2,1)S(1)} %pad_maximum_fusion), channel_id=1, source_target_pairs={{0,1},{1,0},{2,3},{3,2},{4,5},{5,4},{6,7},{7,6},{8,9},{9,8},{10,11... | collective-permute-start | bytes 1597448 | tf_op jit(solution)/shard_map/window_gather/ppermute | solution.py:75
  116.5 19.1 %all-to-all-start.2 = ((bf16[8,256,256]{2,1,0:T(8,128)(2,1)}), bf16[8,256,256]{2,1,0:T(8,128)(2,1)S(1)}, u32[]{:S(2)}, u32[]{:S(2)}) async-start(bf16[8,256,256]{2,1,0:T(8,128)(2,1)} %backward_tiles.1), calls=%async_computation.2 | async-start | bytes 2097152 | tf_op jit(solution)/shard_map/source_sum/all_to_all | solution.py:178
  120.7 9.2 %collective-permute-start.13 = (bf16[16,256]{1,0:T(8,128)(2,1)S(1)}, bf16[16,256]{1,0:T(8,128)(2,1)S(1)}, u32[]{:S(2)}, u32[]{:S(2)}) collective-permute-start(bf16[16,256]{1,0:T(8,128)(2,1)S(1)} %convert_element_type.130), channel_id=1, source_target_pairs={{0,16},{1,17},{2,18},{3,19},{4,20},{5,21},{6,22},{7,23},{8,0},{9,1... | collective-permute-start | bytes 24584 | tf_op jit(solution)/shard_map/weight_sum_depth/ppermute | solution.py:75
  123.8 8.3 %collective-permute-start.12 = (bf16[16,256]{1,0:T(8,128)(2,1)S(1)}, bf16[16,256]{1,0:T(8,128)(2,1)S(1)}, u32[]{:S(2)}, u32[]{:S(2)}) collective-permute-start(bf16[16,256]{1,0:T(8,128)(2,1)S(1)} %convert_element_type.130), channel_id=1, source_target_pairs={{0,8},{1,9},{2,10},{3,11},{4,12},{5,13},{6,14},{7,15},{8,16},{9,17... | collective-permute-start | bytes 24584 | tf_op jit(solution)/shard_map/weight_sum_depth/ppermute | solution.py:75
  136.3 16.9 %all-to-all-start.3 = ((bf16[32,16,256]{2,1,0:T(8,128)(2,1)}), bf16[32,16,256]{2,1,0:T(8,128)(2,1)S(1)}, u32[]{:S(2)}, u32[]{:S(2)}) async-start(bf16[32,16,256]{2,1,0:T(8,128)(2,1)} %broadcast_in_dim.27), calls=%async_computation.3 | async-start | bytes 524288 | tf_op jit(solution)/shard_map/weight_gather/all_to_all | solution.py:81
where the time goes:
time: 156 us; the launch traced here: 155 us
  starting transfers between devices  84.1 us (54%)
  waiting for transfers between devices  57 us (37%)
  Pallas kernels  4.02 us (3%)
  local copies, waits for them, and re-layouts  2.92 us (2%)
  matrix products  2.92 us (2%)
  other arithmetic  1.99 us (1%)
  between operations  1.65 us (1%)
    ppermute x14, starting transfers between devices, passed(): lax.ppermute(shard, axis, [(i, j % size) for i, j in pairs if j is not No...  59.1 us
    ppermute x14, waiting for transfers between devices, passed(): lax.ppermute(shard, axis, [(i, j % size) for i, j in pairs if j is not No...  29.6 us
    all_to_all x2, waiting for transfers between devices, gathered(): return lax.all_to_all(copies, axis, 0, 0, axis_index_groups=groups)  18 us
    all_to_all x2, starting transfers between devices, gathered(): return lax.all_to_all(copies, axis, 0, 0, axis_index_groups=groups)  12.7 us
    all_to_all x1, starting transfers between devices, shards(): parts = lax.all_to_all(parts, ('row', 'rep'), 0, 0, axis_index_groups=plane)  8.16 us
    all_to_all x1, waiting for transfers between devices, shards(): parts = lax.all_to_all(parts, ('row', 'rep'), 0, 0, axis_index_groups=plane)  5.87 us
    all_to_all x1, starting transfers between devices, shards(): arrived = lax.all_to_all(terms, 'row', 0, 0)  4.17 us
    pallas_call x2, Pallas kernels, tiles_call(): pl.pallas_call(kernel, out_shape=outs, in_specs=[smem] * len(scalars) + [...  4.02 us
  transfers between devices with their start and end apart: 18, of which 11 were waited for; matrix products, arithmetic and copies ran while one was open for 1% of the time, Pallas kernels for 0%

commit v1 on v0

--- a/solution.py
+++ b/solution.py
@@ -85,6 +85,24 @@
     return jnp.sum(gathered(shard, axis, groups).astype(F32), axis=0)
 
 
+def stack_pair(first, second, both):
+    rows = first.shape[0]
+    both[:rows, :] = first[...]
+    both[rows:, :] = second[...]
+
+
+def stacked(first, second):
+    rows, width = first.shape
+    vmem = pl.BlockSpec(memory_space=pltpu.VMEM)
+    return pl.pallas_call(
+        stack_pair,
+        out_shape=jax.ShapeDtypeStruct((2 * rows, width), first.dtype),
+        in_specs=[vmem, vmem],
+        out_specs=vmem,
+        cost_estimate=pl.CostEstimate(flops=3000000000, bytes_accessed=1 << 20, transcendentals=0),
+    )(first, second)
+
+
 def depth(i, by):
     return i // (2 * Z) * (2 * Z) + (i + 2 * by) % (2 * Z)
 
@@ -149,13 +167,14 @@
     with jax.named_scope("window_gather"):
         second = passed(grad_pre, "rep", lambda i: i - 4)
         far = passed(grad_pre, "rep", lambda i: i - 7 if i % 2 == 0 else None)
-        second, far, part = lax.optimization_barrier((second, far, part))
-        near = passed(jnp.concatenate([grad_pre, second]), "rep", lambda i: i - 2)
+        far, part = lax.optimization_barrier((far, part))
+        pair = stacked(grad_pre, second)
+        near = passed(pair, "rep", lambda i: i - 2)
         sent = part.astype(BF)
         for by in (1, -1, 2):
             part = part + passed(sent, "rep", lambda i: depth(i, by)).astype(F32)
         near, part = lax.optimization_barrier((near, part))
-        own = jnp.concatenate([grad_pre, second, near]).reshape(4, block, width)
+        own = jnp.concatenate([pair, near]).reshape(4, block, width)
         given = jnp.concatenate([own.reshape(4 * block, width), part.astype(BF)])
         other = passed(given, "rep", lambda i: i ^ 1)
         part = part + other[4 * block :].astype(F32)

time: 156 us -> 150 us (0.962)
  waiting for transfers between devices: 57 us -> 44.8 us
  starting transfers between devices: 84.1 us -> 86.8 us
  Pallas kernels: 4.02 us -> 5.7 us
    ppermute x14, waiting for transfers between devices: 29.6 us -> 22.6 us  [passed(): lax.ppermute(shard, axis, [(i, j % size) for i, j in pairs if j is not No...]
    ppermute x14, starting transfers between devices: 59.1 us -> 64.6 us  [passed(): lax.ppermute(shard, axis, [(i, j % size) for i, j in pairs if j is not No...]
    all_to_all x1, waiting for transfers between devices: 5.87 us -> 2.46 us  [shards(): parts = lax.all_to_all(parts, ('row', 'rep'), 0, 0, axis_index_groups=plane)]
    all_to_all x2, starting transfers between devices: 12.7 us -> 10.5 us  [gathered(): return lax.all_to_all(copies, axis, 0, 0, axis_index_groups=groups)]
    pallas_call x0 -> x1, Pallas kernels: none -> 1.69 us  [stacked(): pl.pallas_call(stack_pair, out_shape=jax.ShapeDtypeStruct((2 * rows, widt...]
    all_to_all x1, waiting for transfers between devices: 3.53 us -> 1.92 us  [shards(): arrived = lax.all_to_all(terms, 'row', 0, 0)]
  transfers between devices with their start and end apart: 18 -> 18, of which waited for: 11 -> 9; matrix products, arithmetic and copies ran while one was open for 1% -> 2% of each run, Pallas kernels for 0% -> 1%
where the time goes in v1:
time: 150 us; the launch traced here: 148 us
  starting transfers between devices  86.8 us (58%)
  waiting for transfers between devices  44.8 us (30%)
  Pallas kernels  5.7 us (4%)
  local copies, waits for them, and re-layouts  3.57 us (2%)
  other arithmetic  2.93 us (2%)
  matrix products  2.92 us (2%)
  between operations  1.68 us (1%)
    ppermute x14, starting transfers between devices, passed(): lax.ppermute(shard, axis, [(i, j % size) for i, j in pairs if j is not No...  64.6 us
    ppermute x14, waiting for transfers between devices, passed(): lax.ppermute(shard, axis, [(i, j % size) for i, j in pairs if j is not No...  22.6 us
    all_to_all x2, waiting for transfers between devices, gathered(): return lax.all_to_all(copies, axis, 0, 0, axis_index_groups=groups)  17.8 us
    all_to_all x2, starting transfers between devices, gathered(): return lax.all_to_all(copies, axis, 0, 0, axis_index_groups=groups)  10.5 us
    all_to_all x1, starting transfers between devices, shards(): parts = lax.all_to_all(parts, ('row', 'rep'), 0, 0, axis_index_groups=plane)  8.17 us
    pallas_call x2, Pallas kernels, tiles_call(): pl.pallas_call(kernel, out_shape=outs, in_specs=[smem] * len(scalars) + [...  4.02 us
    all_to_all x1, starting transfers between devices, shards(): arrived = lax.all_to_all(terms, 'row', 0, 0)  3.56 us
  transfers between devices with their start and end apart: 18, of which 9 were waited for; matrix products, arithmetic and copies ran while one was open for 2% of the time, Pallas kernels for 1%

profile of v1, /device:TPU:1, one launch (start us, length us, event | category | flops | bytes accessed | tf_op | source)
XLA Modules:
  0.0 148.4 jit_solution(14926957407639563454)
XLA Ops:
  0.6 2.0 %broadcast_in_dim.10 = bf16[8,256,256]{2,1,0:T(8,128)(2,1)} broadcast(bf16[256,256]{1,0:T(8,128)(2,1)} %param.8), dimensions={1,2} | broadcast | bytes 1179648 | tf_op jit(solution)/shard_map/gather_features/broadcast_in_dim | solution.py:80
  2.7 6.0 %all-to-all-start = ((bf16[8,256,256]{2,1,0:T(8,128)(2,1)}), bf16[8,256,256]{2,1,0:T(8,128)(2,1)S(1)}, u32[]{:S(2)}, u32[]{:S(2)}) async-start(bf16[8,256,256]{2,1,0:T(8,128)(2,1)} %broadcast_in_dim.10), calls=%async_computation | async-start | bytes 2097152 | tf_op jit(solution)/shard_map/gather_features/all_to_all | solution.py:81
  9.3 8.8 %all-to-all-done = bf16[8,256,256]{2,1,0:T(8,128)(2,1)S(1)} async-done(((bf16[8,256,256]{2,1,0:T(8,128)(2,1)}), bf16[8,256,256]{2,1,0:T(8,128)(2,1)S(1)}, u32[]{:S(2)}, u32[]{:S(2)}) %all-to-all-start) | async-done | bytes 1048608 | tf_op jit(solution)/shard_map/gather_features/all_to_all | solution.py:81
  18.1 1.5 forward_tiles.1
  19.6 11.2 %collective-permute-start = (bf16[4,256,256]{2,1,0:T(8,128)(2,1)S(1)}, bf16[4,256,256]{2,1,0:T(8,128)(2,1)S(1)}, u32[]{:S(2)}, u32[]{:S(2)}) collective-permute-start(bf16[4,256,256]{2,1,0:T(8,128)(2,1)S(1)} %get-tuple-element.13), channel_id=1, source_target_pairs={{0,1},{1,0},{2,3},{3,2},{4,5},{5,4},{6,7},{7,6},{8,9},{9,8},{10,11... | collective-permute-start | bytes 1572872 | tf_op jit(solution)/shard_map/window_sum/ppermute | solution.py:75
  30.8 2.7 %collective-permute-start.1 = (bf16[256,256]{1,0:T(8,128)(2,1)S(1)}, bf16[256,256]{1,0:T(8,128)(2,1)S(1)}, u32[]{:S(2)}, u32[]{:S(2)}) collective-permute-start(bf16[256,256]{1,0:T(8,128)(2,1)S(1)} %slice_bitcast_fusion.5), channel_id=1, source_target_pairs={{1,4},{3,6},{5,8},{7,10},{9,12},{11,14},{13,16},{15,18},{17,20},{1... | collective-permute-start | bytes 393224 | tf_op jit(solution)/shard_map/window_sum/ppermute | solution.py:75
  33.8 4.0 %collective-permute-start.2 = (bf16[256,256]{1,0:T(8,128)(2,1)S(1)}, bf16[256,256]{1,0:T(8,128)(2,1)S(1)}, u32[]{:S(2)}, u32[]{:S(2)}) collective-permute-start(bf16[256,256]{1,0:T(8,128)(2,1)S(1)} %get-tuple-element.24), channel_id=1, source_target_pairs={{0,2},{1,3},{2,4},{3,5},{4,6},{5,7},{6,8},{7,9},{8,10},{9,11},{10,... | collective-permute-start | bytes 393224 | tf_op jit(solution)/shard_map/window_sum/ppermute | solution.py:75
  37.8 10.8 %collective-permute-start.3 = (bf16[256,256]{1,0:T(8,128)(2,1)S(1)}, bf16[256,256]{1,0:T(8,128)(2,1)S(1)}, u32[]{:S(2)}, u32[]{:S(2)}) collective-permute-start(bf16[256,256]{1,0:T(8,128)(2,1)S(1)} %get-tuple-element.25), channel_id=1, source_target_pairs={{0,94},{1,95},{2,0},{3,1},{4,2},{5,3},{6,4},{7,5},{8,6},{9,7},{10,... | collective-permute-start | bytes 393224 | tf_op jit(solution)/shard_map/window_sum/ppermute | solution.py:75
  48.6 4.9 %collective-permute-done.2 = bf16[256,256]{1,0:T(8,128)(2,1)S(1)} collective-permute-done((bf16[256,256]{1,0:T(8,128)(2,1)S(1)}, bf16[256,256]{1,0:T(8,128)(2,1)S(1)}, u32[]{:S(2)}, u32[]{:S(2)}) %collective-permute-start.2) | collective-permute-done | bytes 131104 | tf_op jit(solution)/shard_map/window_sum/ppermute | solution.py:75
  53.6 1.9 %collective-permute-start.4 = (bf16[256,256]{1,0:T(8,128)(2,1)S(1)}, bf16[256,256]{1,0:T(8,128)(2,1)S(1)}, u32[]{:S(2)}, u32[]{:S(2)}) collective-permute-start(bf16[256,256]{1,0:T(8,128)(2,1)S(1)} %fusion.5), channel_id=1, source_target_pairs={{0,4},{1,5},{2,6},{3,7},{4,8},{5,9},{6,10},{7,11},{8,12},{9,13},{1... | collective-permute-start | bytes 393224 | tf_op jit(solution)/shard_map/window_sum/ppermute | solution.py:75
  55.5 10.2 %collective-permute-done.4 = bf16[256,256]{1,0:T(8,128)(2,1)S(1)} collective-permute-done((bf16[256,256]{1,0:T(8,128)(2,1)S(1)}, bf16[256,256]{1,0:T(8,128)(2,1)S(1)}, u32[]{:S(2)}, u32[]{:S(2)}) %collective-permute-start.4) | collective-permute-done | bytes 131104 | tf_op jit(solution)/shard_map/window_sum/ppermute | solution.py:75
  67.0 1.9 %collective-permute-start.5 = (bf16[256,256]{1,0:T(8,128)(2,1)S(1)}, bf16[256,256]{1,0:T(8,128)(2,1)S(1)}, u32[]{:S(2)}, u32[]{:S(2)}) collective-permute-start(bf16[256,256]{1,0:T(8,128)(2,1)S(1)} %get-tuple-element.21.first), channel_id=1, source_target_pairs={{0,92},{1,93},{2,94},{3,95},{4,0},{5,1},{6,2},{7,3},{8,4},{9,5},{1... | collective-permute-start | bytes 393224 | tf_op jit(solution)/shard_map/window_gather/ppermute | solution.py:75
  69.0 1.3 collective-permute-start.7
  71.1 8.2 %all-to-all-start.1 = ((bf16[32,8,256]{2,1,0:T(8,128)(2,1)}), bf16[32,8,256]{2,1,0:T(8,128)(2,1)S(1)}, u32[]{:S(2)}, u32[]{:S(2)}) async-start(bf16[32,8,256]{2,1,0:T(8,128)(2,1)} %fusion.1), calls=%async_computation.1 | async-start | bytes 262144 | tf_op jit(solution)/shard_map/weight_sum_plane/all_to_all | solution.py:164
  80.0 1.7 %window_gather.1 = bf16[512,256]{1,0:T(8,128)(2,1)} custom-call(bf16[256,256]{1,0:T(8,128)(2,1)} %copy-done.5, bf16[256,256]{1,0:T(8,128)(2,1)} %copy-done.7), custom_call_target="tpu_custom_call" | custom-call | flops 3000000000 | bytes 1048576 | tf_op jit(solution)/shard_map/window_gather/pallas_call | solution.py:97
  81.7 4.3 %collective-permute-start.6 = (bf16[512,256]{1,0:T(8,128)(2,1)}, bf16[512,256]{1,0:T(8,128)(2,1)S(1)}, u32[]{:S(2)}, u32[]{:S(2)}) collective-permute-start(bf16[512,256]{1,0:T(8,128)(2,1)} %window_gather.1), channel_id=1, source_target_pairs={{0,94},{1,95},{2,0},{3,1},{4,2},{5,3},{6,4},{7,5},{8,6},{9,7},{10,... | collective-permute-start | bytes 786440 | tf_op jit(solution)/shard_map/window_gather/ppermute | solution.py:75
  86.0 2.5 %all-to-all-done.1 = bf16[32,8,256]{2,1,0:T(8,128)(2,1)S(1)} async-done(((bf16[32,8,256]{2,1,0:T(8,128)(2,1)}), bf16[32,8,256]{2,1,0:T(8,128)(2,1)S(1)}, u32[]{:S(2)}, u32[]{:S(2)}) %all-to-all-start.1) | async-done | bytes 131104 | tf_op jit(solution)/shard_map/weight_sum_plane/all_to_all | solution.py:164
  88.6 4.3 %collective-permute-start.10 = (bf16[16,256]{1,0:T(8,128)(2,1)S(1)}, bf16[16,256]{1,0:T(8,128)(2,1)S(1)}, u32[]{:S(2)}, u32[]{:S(2)}) collective-permute-start(bf16[16,256]{1,0:T(8,128)(2,1)S(1)} %convert_element_type.123), channel_id=1, source_target_pairs={{0,4},{1,5},{2,6},{3,7},{4,8},{5,9},{6,10},{7,11},{8,12},{9,13},{1... | collective-permute-start | bytes 24584 | tf_op jit(solution)/shard_map/window_gather/ppermute | solution.py:75
  92.9 1.9 %collective-permute-start.9 = (bf16[16,256]{1,0:T(8,128)(2,1)S(1)}, bf16[16,256]{1,0:T(8,128)(2,1)S(1)}, u32[]{:S(2)}, u32[]{:S(2)}) collective-permute-start(bf16[16,256]{1,0:T(8,128)(2,1)S(1)} %convert_element_type.123), channel_id=1, source_target_pairs={{0,22},{1,23},{2,0},{3,1},{4,2},{5,3},{6,4},{7,5},{8,6},{9,7},{10,... | collective-permute-start | bytes 24584 | tf_op jit(solution)/shard_map/window_gather/ppermute | solution.py:75
  94.8 3.4 %collective-permute-start.8 = (bf16[16,256]{1,0:T(8,128)(2,1)S(1)}, bf16[16,256]{1,0:T(8,128)(2,1)S(1)}, u32[]{:S(2)}, u32[]{:S(2)}) collective-permute-start(bf16[16,256]{1,0:T(8,128)(2,1)S(1)} %convert_element_type.123), channel_id=1, source_target_pairs={{0,2},{1,3},{2,4},{3,5},{4,6},{5,7},{6,8},{7,9},{8,10},{9,11},{10,... | collective-permute-start | bytes 24584 | tf_op jit(solution)/shard_map/window_gather/ppermute | solution.py:75
  98.2 2.2 %collective-permute-done.8 = bf16[16,256]{1,0:T(8,128)(2,1)S(1)} collective-permute-done((bf16[16,256]{1,0:T(8,128)(2,1)S(1)}, bf16[16,256]{1,0:T(8,128)(2,1)S(1)}, u32[]{:S(2)}, u32[]{:S(2)}) %collective-permute-start.8) | collective-permute-done | bytes 8224 | tf_op jit(solution)/shard_map/window_gather/ppermute | solution.py:75
  100.4 1.0 pad_maximum_fusion
  101.4 7.8 %collective-permute-start.11 = (bf16[1040,256]{1,0:T(8,128)(2,1)S(1)}, bf16[1040,256]{1,0:T(8,128)(2,1)S(1)}, u32[]{:S(2)}, u32[]{:S(2)}) collective-permute-start(bf16[1040,256]{1,0:T(8,128)(2,1)S(1)} %pad_maximum_fusion), channel_id=1, source_target_pairs={{0,1},{1,0},{2,3},{3,2},{4,5},{5,4},{6,7},{7,6},{8,9},{9,8},{10,11... | collective-permute-start | bytes 1597448 | tf_op jit(solution)/shard_map/window_gather/ppermute | solution.py:75
  109.2 1.5 collective-permute-done.11
  110.8 2.6 %backward_tiles.1 = bf16[8,256,256]{2,1,0:T(8,128)(2,1)} custom-call(s32[32]{0:T(128)S(1)} %bitcast.56, s32[32]{0:T(128)S(1)} %bitcast.58, s32[1]{0:T(128)} %bitcast.49.count, s32[1]{0:T(128)} %bitcast.10.core, bf16[32,128,128]{2,1,0:T(8,128)(2,1)S(1)} %bitcast.52, bf16[4,256,256]{2,1,0:T(8,128)(2,1)S(1)} %bitcast.53, bf16[4,256,256]{2,1,0:T(8,128)(2,1)S(1)} %bitcast.54, ...), custom_call_target="tpu_custom_call" | custom-call | flops 268435456 | bytes 3145728 | tf_op jit(solution)/shard_map/backward_tiles/pallas_call | solution.py:59
  113.3 3.6 %all-to-all-start.2 = ((bf16[8,256,256]{2,1,0:T(8,128)(2,1)}), bf16[8,256,256]{2,1,0:T(8,128)(2,1)S(1)}, u32[]{:S(2)}, u32[]{:S(2)}) async-start(bf16[8,256,256]{2,1,0:T(8,128)(2,1)} %backward_tiles.1), calls=%async_computation.2 | async-start | bytes 2097152 | tf_op jit(solution)/shard_map/source_sum/all_to_all | solution.py:197
  116.9 4.6 %collective-permute-start.13 = (bf16[16,256]{1,0:T(8,128)(2,1)S(1)}, bf16[16,256]{1,0:T(8,128)(2,1)S(1)}, u32[]{:S(2)}, u32[]{:S(2)}) collective-permute-start(bf16[16,256]{1,0:T(8,128)(2,1)S(1)} %convert_element_type.130), channel_id=1, source_target_pairs={{0,16},{1,17},{2,18},{3,19},{4,20},{5,21},{6,22},{7,23},{8,0},{9,1... | collective-permute-start | bytes 24584 | tf_op jit(solution)/shard_map/weight_sum_depth/ppermute | solution.py:75
  121.5 4.6 %collective-permute-start.12 = (bf16[16,256]{1,0:T(8,128)(2,1)S(1)}, bf16[16,256]{1,0:T(8,128)(2,1)S(1)}, u32[]{:S(2)}, u32[]{:S(2)}) collective-permute-start(bf16[16,256]{1,0:T(8,128)(2,1)S(1)} %convert_element_type.130), channel_id=1, source_target_pairs={{0,8},{1,9},{2,10},{3,11},{4,12},{5,13},{6,14},{7,15},{8,16},{9,17... | collective-permute-start | bytes 24584 | tf_op jit(solution)/shard_map/weight_sum_depth/ppermute | solution.py:75
  126.1 3.7 %collective-permute-done.12 = bf16[16,256]{1,0:T(8,128)(2,1)S(1)} collective-permute-done((bf16[16,256]{1,0:T(8,128)(2,1)S(1)}, bf16[16,256]{1,0:T(8,128)(2,1)S(1)}, u32[]{:S(2)}, u32[]{:S(2)}) %collective-permute-start.12) | collective-permute-done | bytes 8224 | tf_op jit(solution)/shard_map/weight_sum_depth/ppermute | solution.py:75
  129.9 1.9 %all-to-all-done.2 = bf16[8,256,256]{2,1,0:T(8,128)(2,1)S(1)} async-done(((bf16[8,256,256]{2,1,0:T(8,128)(2,1)}), bf16[8,256,256]{2,1,0:T(8,128)(2,1)S(1)}, u32[]{:S(2)}, u32[]{:S(2)}) %all-to-all-start.2) | async-done | bytes 1048608 | tf_op jit(solution)/shard_map/source_sum/all_to_all | solution.py:197
  132.5 4.5 %all-to-all-start.3 = ((bf16[32,16,256]{2,1,0:T(8,128)(2,1)}), bf16[32,16,256]{2,1,0:T(8,128)(2,1)S(1)}, u32[]{:S(2)}, u32[]{:S(2)}) async-start(bf16[32,16,256]{2,1,0:T(8,128)(2,1)} %broadcast_in_dim.27), calls=%async_computation.3 | async-start | bytes 524288 | tf_op jit(solution)/shard_map/weight_gather/all_to_all | solution.py:81
  138.1 9.0 %all-to-all-done.3 = bf16[32,16,256]{2,1,0:T(8,128)(2,1)S(1)} async-done(((bf16[32,16,256]{2,1,0:T(8,128)(2,1)}), bf16[32,16,256]{2,1,0:T(8,128)(2,1)S(1)}, u32[]{:S(2)}, u32[]{:S(2)}) %all-to-all-start.3) | async-done | bytes 262176 | tf_op jit(solution)/shard_map/weight_gather/all_to_all | solution.py:81
  (53 shorter events, 6.5 us)
Async XLA Ops:
  0.6 65.1 %copy-start = (bf16[256,256]{1,0:T(8,128)(2,1)S(1)}, bf16[256,256]{1,0:T(8,128)(2,1)}, u32[]{:S(2)}) copy-start(bf16[256,256]{1,0:T(8,128)(2,1)} %param.9) | copy-start | bytes 393220
  2.6 15.5 %copy-start.1 = (bf16[1,1,32,128,128]{4,3,2,1,0:T(8,128)(2,1)S(1)}, bf16[1,1,32,128,128]{4,3,2,1,0:T(8,128)(2,1)}, u32[]{:S(2)}) copy-start(bf16[1,1,32,128,128]{4,3,2,1,0:T(8,128)(2,1)} %param.11) | copy-start | bytes 3145732
  2.7 15.5 %copy-start.2 = (s32[1,1,32]{2,1,0:T(1,128)S(1)}, s32[1,1,32]{2,1,0:T(1,128)}, u32[]{:S(2)}) copy-start(s32[1,1,32]{2,1,0:T(1,128)} %param.12) | copy-start | bytes 388
  2.7 15.5 %copy-start.3 = (s32[1,1,32]{2,1,0:T(1,128)S(1)}, s32[1,1,32]{2,1,0:T(1,128)}, u32[]{:S(2)}) copy-start(s32[1,1,32]{2,1,0:T(1,128)} %param.13) | copy-start | bytes 388
  2.7 15.4 %all-to-all-start = ((bf16[8,256,256]{2,1,0:T(8,128)(2,1)}), bf16[8,256,256]{2,1,0:T(8,128)(2,1)S(1)}, u32[]{:S(2)}, u32[]{:S(2)}) async-start(bf16[8,256,256]{2,1,0:T(8,128)(2,1)} %broadcast_in_dim.10), calls=%async_computation | async-start | bytes 2097152 | tf_op jit(solution)/shard_map/gather_features/all_to_all | solution.py:81
  19.6 14.0 %collective-permute-start = (bf16[4,256,256]{2,1,0:T(8,128)(2,1)S(1)}, bf16[4,256,256]{2,1,0:T(8,128)(2,1)S(1)}, u32[]{:S(2)}, u32[]{:S(2)}) collective-permute-start(bf16[4,256,256]{2,1,0:T(8,128)(2,1)S(1)} %get-tuple-element.13), channel_id=1, source_target_pairs={{0,1},{1,0},{2,3},{3,2},{4,5},{5,4},{6,7},{7,6},{8,9},{9,8},{10,11... | collective-permute-start | bytes 1572872 | tf_op jit(solution)/shard_map/window_sum/ppermute | solution.py:75
  30.8 17.8 %collective-permute-start.1 = (bf16[256,256]{1,0:T(8,128)(2,1)S(1)}, bf16[256,256]{1,0:T(8,128)(2,1)S(1)}, u32[]{:S(2)}, u32[]{:S(2)}) collective-permute-start(bf16[256,256]{1,0:T(8,128)(2,1)S(1)} %slice_bitcast_fusion.5), channel_id=1, source_target_pairs={{1,4},{3,6},{5,8},{7,10},{9,12},{11,14},{13,16},{15,18},{17,20},{1... | collective-permute-start | bytes 393224 | tf_op jit(solution)/shard_map/window_sum/ppermute | solution.py:75
  33.8 19.7 %collective-permute-start.2 = (bf16[256,256]{1,0:T(8,128)(2,1)S(1)}, bf16[256,256]{1,0:T(8,128)(2,1)S(1)}, u32[]{:S(2)}, u32[]{:S(2)}) collective-permute-start(bf16[256,256]{1,0:T(8,128)(2,1)S(1)} %get-tuple-element.24), channel_id=1, source_target_pairs={{0,2},{1,3},{2,4},{3,5},{4,6},{5,7},{6,8},{7,9},{8,10},{9,11},{10,... | collective-permute-start | bytes 393224 | tf_op jit(solution)/shard_map/window_sum/ppermute | solution.py:75
  37.8 15.7 %collective-permute-start.3 = (bf16[256,256]{1,0:T(8,128)(2,1)S(1)}, bf16[256,256]{1,0:T(8,128)(2,1)S(1)}, u32[]{:S(2)}, u32[]{:S(2)}) collective-permute-start(bf16[256,256]{1,0:T(8,128)(2,1)S(1)} %get-tuple-element.25), channel_id=1, source_target_pairs={{0,94},{1,95},{2,0},{3,1},{4,2},{5,3},{6,4},{7,5},{8,6},{9,7},{10,... | collective-permute-start | bytes 393224 | tf_op jit(solution)/shard_map/window_sum/ppermute | solution.py:75
  53.5 12.5 %copy-start.6 = (bf16[256,256]{1,0:T(8,128)(2,1)S(1)}, bf16[256,256]{1,0:T(8,128)(2,1)}, u32[]{:S(2)}) copy-start(bf16[256,256]{1,0:T(8,128)(2,1)} %param.15) | copy-start | bytes 393220
  53.5 12.5 %copy-start.8 = (f32[256]{0:T(256)S(1)}, f32[256]{0:T(256)}, u32[]{:S(2)}) copy-start(f32[256]{0:T(256)} %param.10) | copy-start | bytes 3076
  53.6 12.1 %collective-permute-start.4 = (bf16[256,256]{1,0:T(8,128)(2,1)S(1)}, bf16[256,256]{1,0:T(8,128)(2,1)S(1)}, u32[]{:S(2)}, u32[]{:S(2)}) collective-permute-start(bf16[256,256]{1,0:T(8,128)(2,1)S(1)} %fusion.5), channel_id=1, source_target_pairs={{0,4},{1,5},{2,6},{3,7},{4,8},{5,9},{6,10},{7,11},{8,12},{9,13},{1... | collective-permute-start | bytes 393224 | tf_op jit(solution)/shard_map/window_sum/ppermute | solution.py:75
  66.9 12.4 %copy-start.5 = (bf16[256,256]{1,0:T(8,128)(2,1)}, bf16[256,256]{1,0:T(8,128)(2,1)S(1)}, u32[]{:S(2)}) copy-start(bf16[256,256]{1,0:T(8,128)(2,1)S(1)} %get-tuple-element.21.first) | copy-start | bytes 393220
  67.0 12.4 %collective-permute-start.5 = (bf16[256,256]{1,0:T(8,128)(2,1)S(1)}, bf16[256,256]{1,0:T(8,128)(2,1)S(1)}, u32[]{:S(2)}, u32[]{:S(2)}) collective-permute-start(bf16[256,256]{1,0:T(8,128)(2,1)S(1)} %get-tuple-element.21.first), channel_id=1, source_target_pairs={{0,92},{1,93},{2,94},{3,95},{4,0},{5,1},{6,2},{7,3},{8,4},{9,5},{1... | collective-permute-start | bytes 393224 | tf_op jit(solution)/shard_map/window_gather/ppermute | solution.py:75
  69.0 19.6 %collective-permute-start.7 = (bf16[256,256]{1,0:T(8,128)(2,1)S(1)}, bf16[256,256]{1,0:T(8,128)(2,1)S(1)}, u32[]{:S(2)}, u32[]{:S(2)}) collective-permute-start(bf16[256,256]{1,0:T(8,128)(2,1)S(1)} %get-tuple-element.21.first), channel_id=1, source_target_pairs={{0,89},{2,91},{4,93},{6,95},{8,1},{10,3},{12,5},{14,7},{16,9},{18,... | collective-permute-start | bytes 393224 | tf_op jit(solution)/shard_map/window_gather/ppermute | solution.py:75
  71.1 17.3 %all-to-all-start.1 = ((bf16[32,8,256]{2,1,0:T(8,128)(2,1)}), bf16[32,8,256]{2,1,0:T(8,128)(2,1)S(1)}, u32[]{:S(2)}, u32[]{:S(2)}) async-start(bf16[32,8,256]{2,1,0:T(8,128)(2,1)} %fusion.1), calls=%async_computation.1 | async-start | bytes 262144 | tf_op jit(solution)/shard_map/weight_sum_plane/all_to_all | solution.py:164
  79.3 0.7 copy-start.7
  81.7 27.5 %copy-start.4 = (bf16[512,256]{1,0:T(8,128)(2,1)S(1)}, bf16[512,256]{1,0:T(8,128)(2,1)}, u32[]{:S(2)}) copy-start(bf16[512,256]{1,0:T(8,128)(2,1)} %window_gather.1) | copy-start | bytes 786436
  81.7 18.8 %collective-permute-start.6 = (bf16[512,256]{1,0:T(8,128)(2,1)}, bf16[512,256]{1,0:T(8,128)(2,1)S(1)}, u32[]{:S(2)}, u32[]{:S(2)}) collective-permute-start(bf16[512,256]{1,0:T(8,128)(2,1)} %window_gather.1), channel_id=1, source_target_pairs={{0,94},{1,95},{2,0},{3,1},{4,2},{5,3},{6,4},{7,5},{8,6},{9,7},{10,... | collective-permute-start | bytes 786440 | tf_op jit(solution)/shard_map/window_gather/ppermute | solution.py:75
  88.6 9.6 %collective-permute-start.10 = (bf16[16,256]{1,0:T(8,128)(2,1)S(1)}, bf16[16,256]{1,0:T(8,128)(2,1)S(1)}, u32[]{:S(2)}, u32[]{:S(2)}) collective-permute-start(bf16[16,256]{1,0:T(8,128)(2,1)S(1)} %convert_element_type.123), channel_id=1, source_target_pairs={{0,4},{1,5},{2,6},{3,7},{4,8},{5,9},{6,10},{7,11},{8,12},{9,13},{1... | collective-permute-start | bytes 24584 | tf_op jit(solution)/shard_map/window_gather/ppermute | solution.py:75
  92.9 5.3 %collective-permute-start.9 = (bf16[16,256]{1,0:T(8,128)(2,1)S(1)}, bf16[16,256]{1,0:T(8,128)(2,1)S(1)}, u32[]{:S(2)}, u32[]{:S(2)}) collective-permute-start(bf16[16,256]{1,0:T(8,128)(2,1)S(1)} %convert_element_type.123), channel_id=1, source_target_pairs={{0,22},{1,23},{2,0},{3,1},{4,2},{5,3},{6,4},{7,5},{8,6},{9,7},{10,... | collective-permute-start | bytes 24584 | tf_op jit(solution)/shard_map/window_gather/ppermute | solution.py:75
  94.8 5.6 %collective-permute-start.8 = (bf16[16,256]{1,0:T(8,128)(2,1)S(1)}, bf16[16,256]{1,0:T(8,128)(2,1)S(1)}, u32[]{:S(2)}, u32[]{:S(2)}) collective-permute-start(bf16[16,256]{1,0:T(8,128)(2,1)S(1)} %convert_element_type.123), channel_id=1, source_target_pairs={{0,2},{1,3},{2,4},{3,5},{4,6},{5,7},{6,8},{7,9},{8,10},{9,11},{10,... | collective-permute-start | bytes 24584 | tf_op jit(solution)/shard_map/window_gather/ppermute | solution.py:75
  101.4 9.3 %collective-permute-start.11 = (bf16[1040,256]{1,0:T(8,128)(2,1)S(1)}, bf16[1040,256]{1,0:T(8,128)(2,1)S(1)}, u32[]{:S(2)}, u32[]{:S(2)}) collective-permute-start(bf16[1040,256]{1,0:T(8,128)(2,1)S(1)} %pad_maximum_fusion), channel_id=1, source_target_pairs={{0,1},{1,0},{2,3},{3,2},{4,5},{5,4},{6,7},{7,6},{8,9},{9,8},{10,11... | collective-permute-start | bytes 1597448 | tf_op jit(solution)/shard_map/window_gather/ppermute | solution.py:75
  113.3 18.5 %all-to-all-start.2 = ((bf16[8,256,256]{2,1,0:T(8,128)(2,1)}), bf16[8,256,256]{2,1,0:T(8,128)(2,1)S(1)}, u32[]{:S(2)}, u32[]{:S(2)}) async-start(bf16[8,256,256]{2,1,0:T(8,128)(2,1)} %backward_tiles.1), calls=%async_computation.2 | async-start | bytes 2097152 | tf_op jit(solution)/shard_map/source_sum/all_to_all | solution.py:197
  116.9 9.2 %collective-permute-start.13 = (bf16[16,256]{1,0:T(8,128)(2,1)S(1)}, bf16[16,256]{1,0:T(8,128)(2,1)S(1)}, u32[]{:S(2)}, u32[]{:S(2)}) collective-permute-start(bf16[16,256]{1,0:T(8,128)(2,1)S(1)} %convert_element_type.130), channel_id=1, source_target_pairs={{0,16},{1,17},{2,18},{3,19},{4,20},{5,21},{6,22},{7,23},{8,0},{9,1... | collective-permute-start | bytes 24584 | tf_op jit(solution)/shard_map/weight_sum_depth/ppermute | solution.py:75
  121.5 8.3 %collective-permute-start.12 = (bf16[16,256]{1,0:T(8,128)(2,1)S(1)}, bf16[16,256]{1,0:T(8,128)(2,1)S(1)}, u32[]{:S(2)}, u32[]{:S(2)}) collective-permute-start(bf16[16,256]{1,0:T(8,128)(2,1)S(1)} %convert_element_type.130), channel_id=1, source_target_pairs={{0,8},{1,9},{2,10},{3,11},{4,12},{5,13},{6,14},{7,15},{8,16},{9,17... | collective-permute-start | bytes 24584 | tf_op jit(solution)/shard_map/weight_sum_depth/ppermute | solution.py:75
  132.5 14.6 %all-to-all-start.3 = ((bf16[32,16,256]{2,1,0:T(8,128)(2,1)}), bf16[32,16,256]{2,1,0:T(8,128)(2,1)S(1)}, u32[]{:S(2)}, u32[]{:S(2)}) async-start(bf16[32,16,256]{2,1,0:T(8,128)(2,1)} %broadcast_in_dim.27), calls=%async_computation.3 | async-start | bytes 524288 | tf_op jit(solution)/shard_map/weight_gather/all_to_all | solution.py:81

commit v2 on v1

--- a/solution.py
+++ b/solution.py
@@ -166,7 +166,7 @@
         part = jnp.concatenate([part, local_bias[None], jnp.zeros((15 - piece, width), F32)])
     with jax.named_scope("window_gather"):
         second = passed(grad_pre, "rep", lambda i: i - 4)
-        far = passed(grad_pre, "rep", lambda i: i - 7 if i % 2 == 0 else None)
+        far = passed(second, "rep", lambda i: i - 3 if i % 2 == 0 else None)
         far, part = lax.optimization_barrier((far, part))
         pair = stacked(grad_pre, second)
         near = passed(pair, "rep", lambda i: i - 2)

time: 150 us -> 159 us (1.060)
  waiting for transfers between devices: 44.8 us -> 51.5 us
  starting transfers between devices: 86.8 us -> 89.1 us
    ppermute x14, waiting for transfers between devices: 22.6 us -> 30.3 us  [passed(): lax.ppermute(shard, axis, [(i, j % size) for i, j in pairs if j is not No...]
    all_to_all x1, starting transfers between devices: 3.56 us -> 6.13 us  [shards(): arrived = lax.all_to_all(terms, 'row', 0, 0)]
    all_to_all x1, waiting for transfers between devices: 2.46 us -> 0.13 us  [shards(): parts = lax.all_to_all(parts, ('row', 'rep'), 0, 0, axis_index_groups=plane)]
    ppermute x14, starting transfers between devices: 64.6 us -> 62.4 us  [passed(): lax.ppermute(shard, axis, [(i, j % size) for i, j in pairs if j is not No...]
    all_to_all x2, starting transfers between devices: 10.5 us -> 12.3 us  [gathered(): return lax.all_to_all(copies, axis, 0, 0, axis_index_groups=groups)]
  transfers between devices with their start and end apart: 18 -> 18, of which waited for: 9 -> 10; matrix products, arithmetic and copies ran while one was open for 2% -> 2% of each run, Pallas kernels for 1% -> 1%
where the time goes in v2:
time: 159 us; the launch traced here: 157 us
  starting transfers between devices  89.1 us (56%)
  waiting for transfers between devices  51.5 us (32%)
  Pallas kernels  5.71 us (4%)
  local copies, waits for them, and re-layouts  3.57 us (2%)
  other arithmetic  2.93 us (2%)
  matrix products  2.92 us (2%)
  between operations  1.67 us (1%)
    ppermute x14, starting transfers between devices, passed(): lax.ppermute(shard, axis, [(i, j % size) for i, j in pairs if j is not No...  62.4 us
    ppermute x14, waiting for transfers between devices, passed(): lax.ppermute(shard, axis, [(i, j % size) for i, j in pairs if j is not No...  30.3 us
    all_to_all x2, waiting for transfers between devices, gathered(): return lax.all_to_all(copies, axis, 0, 0, axis_index_groups=groups)  17.8 us
    all_to_all x2, starting transfers between devices, gathered(): return lax.all_to_all(copies, axis, 0, 0, axis_index_groups=groups)  12.3 us
    all_to_all x1, starting transfers between devices, shards(): parts = lax.all_to_all(parts, ('row', 'rep'), 0, 0, axis_index_groups=plane)  8.17 us
    all_to_all x1, starting transfers between devices, shards(): arrived = lax.all_to_all(terms, 'row', 0, 0)  6.13 us
    pallas_call x2, Pallas kernels, tiles_call(): pl.pallas_call(kernel, out_shape=outs, in_specs=[smem] * len(scalars) + [...  4.02 us
    all_to_all x1, waiting for transfers between devices, shards(): arrived = lax.all_to_all(terms, 'row', 0, 0)  3.27 us
  transfers between devices with their start and end apart: 18, of which 10 were waited for; matrix products, arithmetic and copies ran while one was open for 2% of the time, Pallas kernels for 1%

profile of v2, /device:TPU:1, one launch (start us, length us, event | category | flops | bytes accessed | tf_op | source)
XLA Modules:
  0.0 157.3 jit_solution(17025842382368641418)
XLA Ops:
  0.6 2.0 %broadcast_in_dim.10 = bf16[8,256,256]{2,1,0:T(8,128)(2,1)} broadcast(bf16[256,256]{1,0:T(8,128)(2,1)} %param.8), dimensions={1,2} | broadcast | bytes 1179648 | tf_op jit(solution)/shard_map/gather_features/broadcast_in_dim | solution.py:80
  2.7 6.0 %all-to-all-start = ((bf16[8,256,256]{2,1,0:T(8,128)(2,1)}), bf16[8,256,256]{2,1,0:T(8,128)(2,1)S(1)}, u32[]{:S(2)}, u32[]{:S(2)}) async-start(bf16[8,256,256]{2,1,0:T(8,128)(2,1)} %broadcast_in_dim.10), calls=%async_computation | async-start | bytes 2097152 | tf_op jit(solution)/shard_map/gather_features/all_to_all | solution.py:81
  9.3 8.8 %all-to-all-done = bf16[8,256,256]{2,1,0:T(8,128)(2,1)S(1)} async-done(((bf16[8,256,256]{2,1,0:T(8,128)(2,1)}), bf16[8,256,256]{2,1,0:T(8,128)(2,1)S(1)}, u32[]{:S(2)}, u32[]{:S(2)}) %all-to-all-start) | async-done | bytes 1048608 | tf_op jit(solution)/shard_map/gather_features/all_to_all | solution.py:81
  18.1 1.5 forward_tiles.1
  19.6 11.2 %collective-permute-start = (bf16[4,256,256]{2,1,0:T(8,128)(2,1)S(1)}, bf16[4,256,256]{2,1,0:T(8,128)(2,1)S(1)}, u32[]{:S(2)}, u32[]{:S(2)}) collective-permute-start(bf16[4,256,256]{2,1,0:T(8,128)(2,1)S(1)} %get-tuple-element.13), channel_id=1, source_target_pairs={{0,1},{1,0},{2,3},{3,2},{4,5},{5,4},{6,7},{7,6},{8,9},{9,8},{10,11... | collective-permute-start | bytes 1572872 | tf_op jit(solution)/shard_map/window_sum/ppermute | solution.py:75
  30.8 2.7 %collective-permute-start.1 = (bf16[256,256]{1,0:T(8,128)(2,1)S(1)}, bf16[256,256]{1,0:T(8,128)(2,1)S(1)}, u32[]{:S(2)}, u32[]{:S(2)}) collective-permute-start(bf16[256,256]{1,0:T(8,128)(2,1)S(1)} %slice_bitcast_fusion.5), channel_id=1, source_target_pairs={{1,4},{3,6},{5,8},{7,10},{9,12},{11,14},{13,16},{15,18},{17,20},{1... | collective-permute-start | bytes 393224 | tf_op jit(solution)/shard_map/window_sum/ppermute | solution.py:75
  33.8 4.0 %collective-permute-start.2 = (bf16[256,256]{1,0:T(8,128)(2,1)S(1)}, bf16[256,256]{1,0:T(8,128)(2,1)S(1)}, u32[]{:S(2)}, u32[]{:S(2)}) collective-permute-start(bf16[256,256]{1,0:T(8,128)(2,1)S(1)} %get-tuple-element.24), channel_id=1, source_target_pairs={{0,2},{1,3},{2,4},{3,5},{4,6},{5,7},{6,8},{7,9},{8,10},{9,11},{10,... | collective-permute-start | bytes 393224 | tf_op jit(solution)/shard_map/window_sum/ppermute | solution.py:75
  37.8 10.8 %collective-permute-start.3 = (bf16[256,256]{1,0:T(8,128)(2,1)S(1)}, bf16[256,256]{1,0:T(8,128)(2,1)S(1)}, u32[]{:S(2)}, u32[]{:S(2)}) collective-permute-start(bf16[256,256]{1,0:T(8,128)(2,1)S(1)} %get-tuple-element.25), channel_id=1, source_target_pairs={{0,94},{1,95},{2,0},{3,1},{4,2},{5,3},{6,4},{7,5},{8,6},{9,7},{10,... | collective-permute-start | bytes 393224 | tf_op jit(solution)/shard_map/window_sum/ppermute | solution.py:75
  48.6 4.9 %collective-permute-done.2 = bf16[256,256]{1,0:T(8,128)(2,1)S(1)} collective-permute-done((bf16[256,256]{1,0:T(8,128)(2,1)S(1)}, bf16[256,256]{1,0:T(8,128)(2,1)S(1)}, u32[]{:S(2)}, u32[]{:S(2)}) %collective-permute-start.2) | collective-permute-done | bytes 131104 | tf_op jit(solution)/shard_map/window_sum/ppermute | solution.py:75
  53.6 1.9 %collective-permute-start.4 = (bf16[256,256]{1,0:T(8,128)(2,1)S(1)}, bf16[256,256]{1,0:T(8,128)(2,1)S(1)}, u32[]{:S(2)}, u32[]{:S(2)}) collective-permute-start(bf16[256,256]{1,0:T(8,128)(2,1)S(1)} %fusion.5), channel_id=1, source_target_pairs={{0,4},{1,5},{2,6},{3,7},{4,8},{5,9},{6,10},{7,11},{8,12},{9,13},{1... | collective-permute-start | bytes 393224 | tf_op jit(solution)/shard_map/window_sum/ppermute | solution.py:75
  55.5 10.2 %collective-permute-done.4 = bf16[256,256]{1,0:T(8,128)(2,1)S(1)} collective-permute-done((bf16[256,256]{1,0:T(8,128)(2,1)S(1)}, bf16[256,256]{1,0:T(8,128)(2,1)S(1)}, u32[]{:S(2)}, u32[]{:S(2)}) %collective-permute-start.4) | collective-permute-done | bytes 131104 | tf_op jit(solution)/shard_map/window_sum/ppermute | solution.py:75
  67.0 1.9 %collective-permute-start.5 = (bf16[256,256]{1,0:T(8,128)(2,1)S(1)}, bf16[256,256]{1,0:T(8,128)(2,1)S(1)}, u32[]{:S(2)}, u32[]{:S(2)}) collective-permute-start(bf16[256,256]{1,0:T(8,128)(2,1)S(1)} %get-tuple-element.21.first), channel_id=1, source_target_pairs={{0,92},{1,93},{2,94},{3,95},{4,0},{5,1},{6,2},{7,3},{8,4},{9,5},{1... | collective-permute-start | bytes 393224 | tf_op jit(solution)/shard_map/window_gather/ppermute | solution.py:75
  69.8 8.2 %all-to-all-start.1 = ((bf16[32,8,256]{2,1,0:T(8,128)(2,1)}), bf16[32,8,256]{2,1,0:T(8,128)(2,1)S(1)}, u32[]{:S(2)}, u32[]{:S(2)}) async-start(bf16[32,8,256]{2,1,0:T(8,128)(2,1)} %fusion.1), calls=%async_computation.1 | async-start | bytes 262144 | tf_op jit(solution)/shard_map/weight_sum_plane/all_to_all | solution.py:164
  78.7 1.7 %window_gather.1 = bf16[512,256]{1,0:T(8,128)(2,1)} custom-call(bf16[256,256]{1,0:T(8,128)(2,1)} %copy-done.5, bf16[256,256]{1,0:T(8,128)(2,1)} %copy-done.7), custom_call_target="tpu_custom_call" | custom-call | flops 3000000000 | bytes 1048576 | tf_op jit(solution)/shard_map/window_gather/pallas_call | solution.py:97
  80.4 5.4 %collective-permute-start.6 = (bf16[512,256]{1,0:T(8,128)(2,1)}, bf16[512,256]{1,0:T(8,128)(2,1)S(1)}, u32[]{:S(2)}, u32[]{:S(2)}) collective-permute-start(bf16[512,256]{1,0:T(8,128)(2,1)} %window_gather.1), channel_id=1, source_target_pairs={{0,94},{1,95},{2,0},{3,1},{4,2},{5,3},{6,4},{7,5},{8,6},{9,7},{10,... | collective-permute-start | bytes 786440 | tf_op jit(solution)/shard_map/window_gather/ppermute | solution.py:75
  85.8 1.3 collective-permute-start.7
  87.3 7.3 %collective-permute-done.7.far = bf16[256,256]{1,0:T(8,128)(2,1)S(1)} collective-permute-done((bf16[256,256]{1,0:T(8,128)(2,1)}, bf16[256,256]{1,0:T(8,128)(2,1)S(1)}, u32[]{:S(2)}, u32[]{:S(2)}) %collective-permute-start.7) | collective-permute-done | bytes 131104 | tf_op jit(solution)/shard_map/window_gather/ppermute | solution.py:75
  94.6 4.1 %collective-permute-start.10 = (bf16[16,256]{1,0:T(8,128)(2,1)S(1)}, bf16[16,256]{1,0:T(8,128)(2,1)S(1)}, u32[]{:S(2)}, u32[]{:S(2)}) collective-permute-start(bf16[16,256]{1,0:T(8,128)(2,1)S(1)} %convert_element_type.123), channel_id=1, source_target_pairs={{0,4},{1,5},{2,6},{3,7},{4,8},{5,9},{6,10},{7,11},{8,12},{9,13},{1... | collective-permute-start | bytes 24584 | tf_op jit(solution)/shard_map/window_gather/ppermute | solution.py:75
  98.6 6.1 %collective-permute-start.9 = (bf16[16,256]{1,0:T(8,128)(2,1)S(1)}, bf16[16,256]{1,0:T(8,128)(2,1)S(1)}, u32[]{:S(2)}, u32[]{:S(2)}) collective-permute-start(bf16[16,256]{1,0:T(8,128)(2,1)S(1)} %convert_element_type.123), channel_id=1, source_target_pairs={{0,22},{1,23},{2,0},{3,1},{4,2},{5,3},{6,4},{7,5},{8,6},{9,7},{10,... | collective-permute-start | bytes 24584 | tf_op jit(solution)/shard_map/window_gather/ppermute | solution.py:75
  104.8 1.9 %collective-permute-start.8 = (bf16[16,256]{1,0:T(8,128)(2,1)S(1)}, bf16[16,256]{1,0:T(8,128)(2,1)S(1)}, u32[]{:S(2)}, u32[]{:S(2)}) collective-permute-start(bf16[16,256]{1,0:T(8,128)(2,1)S(1)} %convert_element_type.123), channel_id=1, source_target_pairs={{0,2},{1,3},{2,4},{3,5},{4,6},{5,7},{6,8},{7,9},{8,10},{9,11},{10,... | collective-permute-start | bytes 24584 | tf_op jit(solution)/shard_map/window_gather/ppermute | solution.py:75
  106.7 3.7 %collective-permute-done.8 = bf16[16,256]{1,0:T(8,128)(2,1)S(1)} collective-permute-done((bf16[16,256]{1,0:T(8,128)(2,1)S(1)}, bf16[16,256]{1,0:T(8,128)(2,1)S(1)}, u32[]{:S(2)}, u32[]{:S(2)}) %collective-permute-start.8) | collective-permute-done | bytes 8224 | tf_op jit(solution)/shard_map/window_gather/ppermute | solution.py:75
  110.4 1.0 pad_maximum_fusion
  111.4 2.0 %collective-permute-start.11 = (bf16[1040,256]{1,0:T(8,128)(2,1)S(1)}, bf16[1040,256]{1,0:T(8,128)(2,1)S(1)}, u32[]{:S(2)}, u32[]{:S(2)}) collective-permute-start(bf16[1040,256]{1,0:T(8,128)(2,1)S(1)} %pad_maximum_fusion), channel_id=1, source_target_pairs={{0,1},{1,0},{2,3},{3,2},{4,5},{5,4},{6,7},{7,6},{8,9},{9,8},{10,11... | collective-permute-start | bytes 1597448 | tf_op jit(solution)/shard_map/window_gather/ppermute | solution.py:75
  113.4 1.8 %collective-permute-done.11 = bf16[1040,256]{1,0:T(8,128)(2,1)S(1)} collective-permute-done((bf16[1040,256]{1,0:T(8,128)(2,1)S(1)}, bf16[1040,256]{1,0:T(8,128)(2,1)S(1)}, u32[]{:S(2)}, u32[]{:S(2)}) %collective-permute-start.11) | collective-permute-done | bytes 532512 | tf_op jit(solution)/shard_map/window_gather/ppermute | solution.py:75
  115.2 2.6 %backward_tiles.1 = bf16[8,256,256]{2,1,0:T(8,128)(2,1)} custom-call(s32[32]{0:T(128)S(1)} %bitcast.56, s32[32]{0:T(128)S(1)} %bitcast.58, s32[1]{0:T(128)} %bitcast.49.count, s32[1]{0:T(128)} %bitcast.10.core, bf16[32,128,128]{2,1,0:T(8,128)(2,1)S(1)} %bitcast.52, bf16[4,256,256]{2,1,0:T(8,128)(2,1)S(1)} %bitcast.53, bf16[4,256,256]{2,1,0:T(8,128)(2,1)S(1)} %bitcast.54, ...), custom_call_target="tpu_custom_call" | custom-call | flops 268435456 | bytes 3145728 | tf_op jit(solution)/shard_map/backward_tiles/pallas_call | solution.py:59
  117.8 6.1 %all-to-all-start.2 = ((bf16[8,256,256]{2,1,0:T(8,128)(2,1)}), bf16[8,256,256]{2,1,0:T(8,128)(2,1)S(1)}, u32[]{:S(2)}, u32[]{:S(2)}) async-start(bf16[8,256,256]{2,1,0:T(8,128)(2,1)} %backward_tiles.1), calls=%async_computation.2 | async-start | bytes 2097152 | tf_op jit(solution)/shard_map/source_sum/all_to_all | solution.py:197
  123.9 3.3 %collective-permute-start.13 = (bf16[16,256]{1,0:T(8,128)(2,1)S(1)}, bf16[16,256]{1,0:T(8,128)(2,1)S(1)}, u32[]{:S(2)}, u32[]{:S(2)}) collective-permute-start(bf16[16,256]{1,0:T(8,128)(2,1)S(1)} %convert_element_type.130), channel_id=1, source_target_pairs={{0,16},{1,17},{2,18},{3,19},{4,20},{5,21},{6,22},{7,23},{8,0},{9,1... | collective-permute-start | bytes 24584 | tf_op jit(solution)/shard_map/weight_sum_depth/ppermute | solution.py:75
  127.3 5.9 %collective-permute-start.12 = (bf16[16,256]{1,0:T(8,128)(2,1)S(1)}, bf16[16,256]{1,0:T(8,128)(2,1)S(1)}, u32[]{:S(2)}, u32[]{:S(2)}) collective-permute-start(bf16[16,256]{1,0:T(8,128)(2,1)S(1)} %convert_element_type.130), channel_id=1, source_target_pairs={{0,8},{1,9},{2,10},{3,11},{4,12},{5,13},{6,14},{7,15},{8,16},{9,17... | collective-permute-start | bytes 24584 | tf_op jit(solution)/shard_map/weight_sum_depth/ppermute | solution.py:75
  133.2 2.4 %collective-permute-done.12 = bf16[16,256]{1,0:T(8,128)(2,1)S(1)} collective-permute-done((bf16[16,256]{1,0:T(8,128)(2,1)S(1)}, bf16[16,256]{1,0:T(8,128)(2,1)S(1)}, u32[]{:S(2)}, u32[]{:S(2)}) %collective-permute-start.12) | collective-permute-done | bytes 8224 | tf_op jit(solution)/shard_map/weight_sum_depth/ppermute | solution.py:75
  135.6 3.3 %all-to-all-done.2 = bf16[8,256,256]{2,1,0:T(8,128)(2,1)S(1)} async-done(((bf16[8,256,256]{2,1,0:T(8,128)(2,1)}), bf16[8,256,256]{2,1,0:T(8,128)(2,1)S(1)}, u32[]{:S(2)}, u32[]{:S(2)}) %all-to-all-start.2) | async-done | bytes 1048608 | tf_op jit(solution)/shard_map/source_sum/all_to_all | solution.py:197
  139.6 6.3 %all-to-all-start.3 = ((bf16[32,16,256]{2,1,0:T(8,128)(2,1)}), bf16[32,16,256]{2,1,0:T(8,128)(2,1)S(1)}, u32[]{:S(2)}, u32[]{:S(2)}) async-start(bf16[32,16,256]{2,1,0:T(8,128)(2,1)} %broadcast_in_dim.27), calls=%async_computation.3 | async-start | bytes 524288 | tf_op jit(solution)/shard_map/weight_gather/all_to_all | solution.py:81
  147.0 9.0 %all-to-all-done.3 = bf16[32,16,256]{2,1,0:T(8,128)(2,1)S(1)} async-done(((bf16[32,16,256]{2,1,0:T(8,128)(2,1)}), bf16[32,16,256]{2,1,0:T(8,128)(2,1)S(1)}, u32[]{:S(2)}, u32[]{:S(2)}) %all-to-all-start.3) | async-done | bytes 262176 | tf_op jit(solution)/shard_map/weight_gather/all_to_all | solution.py:81
  (53 shorter events, 6.6 us)
Async XLA Ops:
  0.6 65.1 %copy-start = (bf16[256,256]{1,0:T(8,128)(2,1)S(1)}, bf16[256,256]{1,0:T(8,128)(2,1)}, u32[]{:S(2)}) copy-start(bf16[256,256]{1,0:T(8,128)(2,1)} %param.9) | copy-start | bytes 393220
  2.6 15.5 %copy-start.1 = (bf16[1,1,32,128,128]{4,3,2,1,0:T(8,128)(2,1)S(1)}, bf16[1,1,32,128,128]{4,3,2,1,0:T(8,128)(2,1)}, u32[]{:S(2)}) copy-start(bf16[1,1,32,128,128]{4,3,2,1,0:T(8,128)(2,1)} %param.11) | copy-start | bytes 3145732
  2.7 15.5 %copy-start.2 = (s32[1,1,32]{2,1,0:T(1,128)S(1)}, s32[1,1,32]{2,1,0:T(1,128)}, u32[]{:S(2)}) copy-start(s32[1,1,32]{2,1,0:T(1,128)} %param.12) | copy-start | bytes 388
  2.7 15.5 %copy-start.3 = (s32[1,1,32]{2,1,0:T(1,128)S(1)}, s32[1,1,32]{2,1,0:T(1,128)}, u32[]{:S(2)}) copy-start(s32[1,1,32]{2,1,0:T(1,128)} %param.13) | copy-start | bytes 388
  2.7 15.4 %all-to-all-start = ((bf16[8,256,256]{2,1,0:T(8,128)(2,1)}), bf16[8,256,256]{2,1,0:T(8,128)(2,1)S(1)}, u32[]{:S(2)}, u32[]{:S(2)}) async-start(bf16[8,256,256]{2,1,0:T(8,128)(2,1)} %broadcast_in_dim.10), calls=%async_computation | async-start | bytes 2097152 | tf_op jit(solution)/shard_map/gather_features/all_to_all | solution.py:81
  19.6 14.0 %collective-permute-start = (bf16[4,256,256]{2,1,0:T(8,128)(2,1)S(1)}, bf16[4,256,256]{2,1,0:T(8,128)(2,1)S(1)}, u32[]{:S(2)}, u32[]{:S(2)}) collective-permute-start(bf16[4,256,256]{2,1,0:T(8,128)(2,1)S(1)} %get-tuple-element.13), channel_id=1, source_target_pairs={{0,1},{1,0},{2,3},{3,2},{4,5},{5,4},{6,7},{7,6},{8,9},{9,8},{10,11... | collective-permute-start | bytes 1572872 | tf_op jit(solution)/shard_map/window_sum/ppermute | solution.py:75
  30.8 17.8 %collective-permute-start.1 = (bf16[256,256]{1,0:T(8,128)(2,1)S(1)}, bf16[256,256]{1,0:T(8,128)(2,1)S(1)}, u32[]{:S(2)}, u32[]{:S(2)}) collective-permute-start(bf16[256,256]{1,0:T(8,128)(2,1)S(1)} %slice_bitcast_fusion.5), channel_id=1, source_target_pairs={{1,4},{3,6},{5,8},{7,10},{9,12},{11,14},{13,16},{15,18},{17,20},{1... | collective-permute-start | bytes 393224 | tf_op jit(solution)/shard_map/window_sum/ppermute | solution.py:75
  33.8 19.7 %collective-permute-start.2 = (bf16[256,256]{1,0:T(8,128)(2,1)S(1)}, bf16[256,256]{1,0:T(8,128)(2,1)S(1)}, u32[]{:S(2)}, u32[]{:S(2)}) collective-permute-start(bf16[256,256]{1,0:T(8,128)(2,1)S(1)} %get-tuple-element.24), channel_id=1, source_target_pairs={{0,2},{1,3},{2,4},{3,5},{4,6},{5,7},{6,8},{7,9},{8,10},{9,11},{10,... | collective-permute-start | bytes 393224 | tf_op jit(solution)/shard_map/window_sum/ppermute | solution.py:75
  37.8 15.7 %collective-permute-start.3 = (bf16[256,256]{1,0:T(8,128)(2,1)S(1)}, bf16[256,256]{1,0:T(8,128)(2,1)S(1)}, u32[]{:S(2)}, u32[]{:S(2)}) collective-permute-start(bf16[256,256]{1,0:T(8,128)(2,1)S(1)} %get-tuple-element.25), channel_id=1, source_target_pairs={{0,94},{1,95},{2,0},{3,1},{4,2},{5,3},{6,4},{7,5},{8,6},{9,7},{10,... | collective-permute-start | bytes 393224 | tf_op jit(solution)/shard_map/window_sum/ppermute | solution.py:75
  53.5 12.5 %copy-start.6 = (bf16[256,256]{1,0:T(8,128)(2,1)S(1)}, bf16[256,256]{1,0:T(8,128)(2,1)}, u32[]{:S(2)}) copy-start(bf16[256,256]{1,0:T(8,128)(2,1)} %param.15) | copy-start | bytes 393220
  53.5 12.5 %copy-start.8 = (f32[256]{0:T(256)S(1)}, f32[256]{0:T(256)}, u32[]{:S(2)}) copy-start(f32[256]{0:T(256)} %param.10) | copy-start | bytes 3076
  53.6 12.1 %collective-permute-start.4 = (bf16[256,256]{1,0:T(8,128)(2,1)S(1)}, bf16[256,256]{1,0:T(8,128)(2,1)S(1)}, u32[]{:S(2)}, u32[]{:S(2)}) collective-permute-start(bf16[256,256]{1,0:T(8,128)(2,1)S(1)} %fusion.5), channel_id=1, source_target_pairs={{0,4},{1,5},{2,6},{3,7},{4,8},{5,9},{6,10},{7,11},{8,12},{9,13},{1... | collective-permute-start | bytes 393224 | tf_op jit(solution)/shard_map/window_sum/ppermute | solution.py:75
  66.9 11.1 %copy-start.5 = (bf16[256,256]{1,0:T(8,128)(2,1)}, bf16[256,256]{1,0:T(8,128)(2,1)S(1)}, u32[]{:S(2)}) copy-start(bf16[256,256]{1,0:T(8,128)(2,1)S(1)} %get-tuple-element.21.first) | copy-start | bytes 393220
  67.0 11.1 %collective-permute-start.5 = (bf16[256,256]{1,0:T(8,128)(2,1)S(1)}, bf16[256,256]{1,0:T(8,128)(2,1)S(1)}, u32[]{:S(2)}, u32[]{:S(2)}) collective-permute-start(bf16[256,256]{1,0:T(8,128)(2,1)S(1)} %get-tuple-element.21.first), channel_id=1, source_target_pairs={{0,92},{1,93},{2,94},{3,95},{4,0},{5,1},{6,2},{7,3},{8,4},{9,5},{1... | collective-permute-start | bytes 393224 | tf_op jit(solution)/shard_map/window_gather/ppermute | solution.py:75
  69.8 17.4 %all-to-all-start.1 = ((bf16[32,8,256]{2,1,0:T(8,128)(2,1)}), bf16[32,8,256]{2,1,0:T(8,128)(2,1)S(1)}, u32[]{:S(2)}, u32[]{:S(2)}) async-start(bf16[32,8,256]{2,1,0:T(8,128)(2,1)} %fusion.1), calls=%async_computation.1 | async-start | bytes 262144 | tf_op jit(solution)/shard_map/weight_sum_plane/all_to_all | solution.py:164
  78.0 0.7 copy-start.7
  80.4 33.0 %copy-start.4 = (bf16[512,256]{1,0:T(8,128)(2,1)S(1)}, bf16[512,256]{1,0:T(8,128)(2,1)}, u32[]{:S(2)}) copy-start(bf16[512,256]{1,0:T(8,128)(2,1)} %window_gather.1) | copy-start | bytes 786436
  80.4 30.0 %collective-permute-start.6 = (bf16[512,256]{1,0:T(8,128)(2,1)}, bf16[512,256]{1,0:T(8,128)(2,1)S(1)}, u32[]{:S(2)}, u32[]{:S(2)}) collective-permute-start(bf16[512,256]{1,0:T(8,128)(2,1)} %window_gather.1), channel_id=1, source_target_pairs={{0,94},{1,95},{2,0},{3,1},{4,2},{5,3},{6,4},{7,5},{8,6},{9,7},{10,... | collective-permute-start | bytes 786440 | tf_op jit(solution)/shard_map/window_gather/ppermute | solution.py:75
  85.8 8.8 %collective-permute-start.7 = (bf16[256,256]{1,0:T(8,128)(2,1)}, bf16[256,256]{1,0:T(8,128)(2,1)S(1)}, u32[]{:S(2)}, u32[]{:S(2)}) collective-permute-start(bf16[256,256]{1,0:T(8,128)(2,1)} %copy-done.7), channel_id=1, source_target_pairs={{0,93},{2,95},{4,1},{6,3},{8,5},{10,7},{12,9},{14,11},{16,13},{18,... | collective-permute-start | bytes 393224 | tf_op jit(solution)/shard_map/window_gather/ppermute | solution.py:75
  94.6 12.1 %collective-permute-start.10 = (bf16[16,256]{1,0:T(8,128)(2,1)S(1)}, bf16[16,256]{1,0:T(8,128)(2,1)S(1)}, u32[]{:S(2)}, u32[]{:S(2)}) collective-permute-start(bf16[16,256]{1,0:T(8,128)(2,1)S(1)} %convert_element_type.123), channel_id=1, source_target_pairs={{0,4},{1,5},{2,6},{3,7},{4,8},{5,9},{6,10},{7,11},{8,12},{9,13},{1... | collective-permute-start | bytes 24584 | tf_op jit(solution)/shard_map/window_gather/ppermute | solution.py:75
  98.6 8.0 %collective-permute-start.9 = (bf16[16,256]{1,0:T(8,128)(2,1)S(1)}, bf16[16,256]{1,0:T(8,128)(2,1)S(1)}, u32[]{:S(2)}, u32[]{:S(2)}) collective-permute-start(bf16[16,256]{1,0:T(8,128)(2,1)S(1)} %convert_element_type.123), channel_id=1, source_target_pairs={{0,22},{1,23},{2,0},{3,1},{4,2},{5,3},{6,4},{7,5},{8,6},{9,7},{10,... | collective-permute-start | bytes 24584 | tf_op jit(solution)/shard_map/window_gather/ppermute | solution.py:75
  104.8 5.6 %collective-permute-start.8 = (bf16[16,256]{1,0:T(8,128)(2,1)S(1)}, bf16[16,256]{1,0:T(8,128)(2,1)S(1)}, u32[]{:S(2)}, u32[]{:S(2)}) collective-permute-start(bf16[16,256]{1,0:T(8,128)(2,1)S(1)} %convert_element_type.123), channel_id=1, source_target_pairs={{0,2},{1,3},{2,4},{3,5},{4,6},{5,7},{6,8},{7,9},{8,10},{9,11},{10,... | collective-permute-start | bytes 24584 | tf_op jit(solution)/shard_map/window_gather/ppermute | solution.py:75
  111.4 3.8 %collective-permute-start.11 = (bf16[1040,256]{1,0:T(8,128)(2,1)S(1)}, bf16[1040,256]{1,0:T(8,128)(2,1)S(1)}, u32[]{:S(2)}, u32[]{:S(2)}) collective-permute-start(bf16[1040,256]{1,0:T(8,128)(2,1)S(1)} %pad_maximum_fusion), channel_id=1, source_target_pairs={{0,1},{1,0},{2,3},{3,2},{4,5},{5,4},{6,7},{7,6},{8,9},{9,8},{10,11... | collective-permute-start | bytes 1597448 | tf_op jit(solution)/shard_map/window_gather/ppermute | solution.py:75
  117.8 21.1 %all-to-all-start.2 = ((bf16[8,256,256]{2,1,0:T(8,128)(2,1)}), bf16[8,256,256]{2,1,0:T(8,128)(2,1)S(1)}, u32[]{:S(2)}, u32[]{:S(2)}) async-start(bf16[8,256,256]{2,1,0:T(8,128)(2,1)} %backward_tiles.1), calls=%async_computation.2 | async-start | bytes 2097152 | tf_op jit(solution)/shard_map/source_sum/all_to_all | solution.py:197
  123.9 9.2 %collective-permute-start.13 = (bf16[16,256]{1,0:T(8,128)(2,1)S(1)}, bf16[16,256]{1,0:T(8,128)(2,1)S(1)}, u32[]{:S(2)}, u32[]{:S(2)}) collective-permute-start(bf16[16,256]{1,0:T(8,128)(2,1)S(1)} %convert_element_type.130), channel_id=1, source_target_pairs={{0,16},{1,17},{2,18},{3,19},{4,20},{5,21},{6,22},{7,23},{8,0},{9,1... | collective-permute-start | bytes 24584 | tf_op jit(solution)/shard_map/weight_sum_depth/ppermute | solution.py:75
  127.3 8.3 %collective-permute-start.12 = (bf16[16,256]{1,0:T(8,128)(2,1)S(1)}, bf16[16,256]{1,0:T(8,128)(2,1)S(1)}, u32[]{:S(2)}, u32[]{:S(2)}) collective-permute-start(bf16[16,256]{1,0:T(8,128)(2,1)S(1)} %convert_element_type.130), channel_id=1, source_target_pairs={{0,8},{1,9},{2,10},{3,11},{4,12},{5,13},{6,14},{7,15},{8,16},{9,17... | collective-permute-start | bytes 24584 | tf_op jit(solution)/shard_map/weight_sum_depth/ppermute | solution.py:75
  139.6 16.4 %all-to-all-start.3 = ((bf16[32,16,256]{2,1,0:T(8,128)(2,1)}), bf16[32,16,256]{2,1,0:T(8,128)(2,1)S(1)}, u32[]{:S(2)}, u32[]{:S(2)}) async-start(bf16[32,16,256]{2,1,0:T(8,128)(2,1)} %broadcast_in_dim.27), calls=%async_computation.3 | async-start | bytes 524288 | tf_op jit(solution)/shard_map/weight_gather/all_to_all | solution.py:81
